TPU v7x, 128 devices: a whole 4x4x4 slice. The times are simulated.
128 devices in a mesh: ctx: 32 (over z_lo, y, x), head: 4 (over z_hi, core).
Axes of the slice: x: 4, y: 4, z: 4 (z_hi: 2, z_lo: 2; z = z_hi * 2 + z_lo), core: 2. Of those that a mesh axis runs over, the one named last changes fastest.
Arguments:
- query: bfloat16 [8192, 4096], P('ctx', 'head'), may hold values from -3 to 3
- key: bfloat16 [8192, 512], P('ctx', 'head'), may hold values from -3 to 3
- value: bfloat16 [8192, 512], P('ctx', 'head'), may hold values from -6 to 6
- attention_out: bfloat16 [8192, 4096], P('ctx', 'head'), may hold values from -6 to 6
- out_grad: bfloat16 [8192, 4096], P('ctx', 'head'), may hold values from -6 to 6
- log_norm: float32 [8192, 32], P('ctx', 'head'), may hold values from 0 to 12
- span_order: int32 [64], P('ctx'), may hold values from 0 to 63, as said below
- span_segment: int32 [64], P('ctx'), may hold values from 0 to 63, as said below
- key_weight: bfloat16 [8192, 512], P(None, 'head'), may hold values from -0.0625 to 0.0625
- value_weight: bfloat16 [8192, 512], P(None, 'head'), may hold values from -0.0625 to 0.0625
Outputs:
- query_grad: bfloat16 [8192, 4096], P('ctx', 'head')
- key_grad: bfloat16 [8192, 512], P('ctx', 'head')
- value_grad: bfloat16 [8192, 512], P('ctx', 'head')
- input_grad: bfloat16 [8192, 8192], P('ctx', 'head')
Inputs may be any that keep to these rules, and one draw needn't show every extreme that they name: `span_order`: each device's two slots hold spans c and 63 - c; every span lies in exactly one slot. `span_segment`: documents are runs of whole spans, each named by the index in the sequence of its first span; the last span of the sequence is a document of its own.
All inputs are finite; a program needn't handle non-finite values.
Results may differ from a plain program's by a relative error of at most 0.018.
Values may be sent and summed in bfloat16 or wider, within the bound.
A program may use at most 64 MiB of HBM per device.

v0:
```python
import math

import jax
import jax.numpy as jnp
from jax import lax
from jax.sharding import PartitionSpec as P

HEAD_DIM = 128
GROUP = 8


def passed_along(block, axis, distance):
    devices = range(lax.axis_size(axis))
    route = [((i - distance) % len(devices), i) for i in devices]
    return lax.ppermute(block, axis, route)


def sweep(members, advance, state):

    def turn(index, carry):
        for inner in range(2):
            carry = advance(2 * index + inner, carry)
        return carry

    return lax.fori_loop(0, members // 2, turn, state)


def per_device(
    query,
    key,
    value,
    attention_out,
    out_grad,
    log_norm,
    span_order,
    span_segment,
    key_weight,
    value_weight,
):
    rows = query.shape[0]
    span = rows // 2
    local_heads = key.shape[1] // HEAD_DIM
    group = GROUP
    scale = 1.0 / math.sqrt(HEAD_DIM)
    members = lax.axis_size("ctx")
    self_index = lax.axis_index("ctx")
    order_all, segment_all = (
        lax.all_gather(span_order, "ctx", axis=0, tiled=True),
        lax.all_gather(span_segment, "ctx", axis=0, tiled=True),
    )
    queries = query.reshape(rows, local_heads, group, HEAD_DIM)
    grads = out_grad.reshape(rows, local_heads, group, HEAD_DIM)
    outputs = attention_out.reshape(rows, local_heads, group, HEAD_DIM)
    delta = jnp.sum(grads.astype(jnp.float32) * outputs.astype(jnp.float32), axis=-1)
    delta_rows = jnp.transpose(delta, (1, 2, 0))[..., None]
    norm_rows = jnp.transpose(log_norm.reshape(rows, local_heads, group), (1, 2, 0))[..., None]
    offsets = jnp.arange(rows, dtype=jnp.int32)
    first_half = offsets < span
    row_position = jnp.where(first_half, span_order[0], span_order[1]) * span + offsets % span
    row_document = jnp.where(first_half, span_segment[0], span_segment[1])
    inner_rows = jnp.arange(span, dtype=jnp.int32)
    query_zero = jnp.zeros((rows, local_heads, group, HEAD_DIM), jnp.float32)

    def dense(operands):
        span_keys, span_values, key_id, key_document = operands
        key_position = key_id * span + inner_rows
        visible = (row_document[:, None] == key_document) & (
            key_position[None, :] <= row_position[:, None]
        )
        scores = (
            jnp.einsum("ihgd,jhd->hgij", queries, span_keys, preferred_element_type=jnp.float32)
            * scale
        )
        attend = jnp.where(visible, jnp.exp(scores - norm_rows), 0.0)
        attend_low = attend.astype(jnp.bfloat16)
        attend_grad = jnp.einsum(
            "ihgd,jhd->hgij", grads, span_values, preferred_element_type=jnp.float32
        )
        score_low = (attend * (attend_grad - delta_rows)).astype(jnp.bfloat16)
        value_part = jnp.einsum(
            "hgij,ihgd->jhd", attend_low, grads, preferred_element_type=jnp.float32
        )
        key_part = (
            jnp.einsum("hgij,ihgd->jhd", score_low, queries, preferred_element_type=jnp.float32)
            * scale
        )
        query_part = (
            jnp.einsum("hgij,jhd->ihgd", score_low, span_keys, preferred_element_type=jnp.float32)
            * scale
        )
        return (query_part, key_part, value_part)

    def span_terms(span_keys, span_values, key_id, key_document):
        operands = (span_keys, span_values, key_id, key_document)
        result = dense(operands)
        return result

    def slot_tables(anchor):
        span_ids = lax.dynamic_slice_in_dim(order_all, 2 * anchor, 2)
        span_documents = lax.dynamic_slice_in_dim(segment_all, 2 * anchor, 2)
        return (span_ids, span_documents)

    def pair_terms(block_keys, block_values, span_ids, span_documents):
        first = span_terms(block_keys[:span], block_values[:span], span_ids[0], span_documents[0])
        second = span_terms(block_keys[span:], block_values[span:], span_ids[1], span_documents[1])
        key_part = jnp.concatenate([first[1], second[1]], axis=0)
        value_part = jnp.concatenate([first[2], second[2]], axis=0)
        return (first[0] + second[0], key_part, value_part)

    keys_local = key.reshape(rows, local_heads, HEAD_DIM)
    values_local = value.reshape(rows, local_heads, HEAD_DIM)
    block_zero = jnp.zeros((rows, local_heads, HEAD_DIM), jnp.float32)

    def advance(step, carry):
        block_keys, block_values, key_acc, value_acc, query_acc = carry
        anchor = (self_index - step) % members
        span_ids, span_documents = slot_tables(anchor)
        query_part, key_part, value_part = pair_terms(
            block_keys, block_values, span_ids, span_documents
        )
        block_keys, block_values = passed_along((block_keys, block_values), "ctx", 1)
        key_acc, value_acc = passed_along((key_acc + key_part, value_acc + value_part), "ctx", 1)
        return (block_keys, block_values, key_acc, value_acc, query_acc + query_part)

    final = sweep(members, advance, (keys_local, values_local, block_zero, block_zero, query_zero))
    key_total = final[2]
    value_total = final[3]
    query_total = final[4]
    query_grad = query_total.reshape(rows, local_heads * group * HEAD_DIM).astype(jnp.bfloat16)
    key_grad = key_total.reshape(rows, local_heads * HEAD_DIM).astype(jnp.bfloat16)
    value_grad = value_total.reshape(rows, local_heads * HEAD_DIM).astype(jnp.bfloat16)
    contract = (((1,), (1,)), ((), ()))
    term = lax.dot_general(key_grad, key_weight, contract, preferred_element_type=jnp.float32)
    term = term + lax.dot_general(
        value_grad, value_weight, contract, preferred_element_type=jnp.float32
    )
    input_grad = lax.psum_scatter(
        term.astype(jnp.bfloat16), "head", scatter_dimension=1, tiled=True
    )
    return (query_grad, key_grad, value_grad, input_grad)


def solution(mesh):
    in_specs = (
        P("ctx", "head"),
        P("ctx", "head"),
        P("ctx", "head"),
        P("ctx", "head"),
        P("ctx", "head"),
        P("ctx", "head"),
        P("ctx"),
        P("ctx"),
        P(None, "head"),
        P(None, "head"),
    )
    out_specs = (P("ctx", "head"), P("ctx", "head"), P("ctx", "head"), P("ctx", "head"))
    return jax.shard_map(
        per_device, mesh=mesh, in_specs=in_specs, out_specs=out_specs, check_vma=False
    )
```

profile of v0, /device:TPU:1, one launch (start us, length us, event | category | flops | bytes accessed | tf_op | source)
XLA Modules:
  0.0 815.2 jit_solution(9033662688276437354)
XLA Ops:
  23.5 17.4 %all-reduce.2 = (s32[64]{0:T(128)}, s32[64]{0:T(128)}) all-reduce(s32[64]{0:T(128)S(1)} %dynamic-update-slice, s32[64]{0:T(128)S(1)} %dynamic-update-slice.1), channel_id=1, replica_groups=mesh['ctx'=32,'head'=4] {'ctx'}, use_global_device_ids=true, to_apply=%add | all-reduce | flops 128 | bytes 1024
  41.0 689.1 %while.25 = (s32[]{:T(128)}, bf16[256,1,128]{2,0,1:T(8,128)(2,1)S(1)}, bf16[256,1,128]{2,0,1:T(8,128)(2,1)}, f32[256,1,128]{2,0,1:T(8,128)S(1)}, f32[256,1,128]{...) while((s32[]{:T(128)}, ...), condition=%wide.region_2.3_spmd.clone.clone, body=%wide.region_1.2_spmd.clone.clone.sunk | while | flops 1351947264 | bytes 54338820 | solution.py:25
  48.7 2.6 select_compare_fusion.6
  89.3 2.6 select_compare_fusion.6
  119.8 3.2 collective-permute-done.5
  131.6 2.6 select_compare_fusion.6
  143.5 2.7 collective-permute-start.6
  155.5 3.1 collective-permute-start.7
  162.5 2.8 collective-permute-done.5
  174.7 2.6 select_compare_fusion.6
  197.8 3.1 collective-permute-start.7
  203.2 3.1 collective-permute-done.5
  206.4 2.8 collective-permute-done.7
  216.4 2.6 select_compare_fusion.6
  242.7 3.7 collective-permute-start.7
  248.5 3.3 collective-permute-done.7
  261.5 2.6 select_compare_fusion.6
  292.7 2.7 collective-permute-done.7
  302.6 2.6 select_compare_fusion.6
  315.5 4.0 collective-permute-start.6
  335.1 4.4 collective-permute-done.5
  339.5 2.8 collective-permute-done.7
  349.6 2.6 select_compare_fusion.6
  379.6 5.6 collective-permute-done.5
  394.8 2.6 select_compare_fusion.6
  419.6 3.4 collective-permute-done.3
  435.1 2.6 select_compare_fusion.6
  447.0 4.2 collective-permute-start.6
  466.8 3.7 collective-permute-done.5
  470.5 2.8 collective-permute-done.7
  480.6 2.6 select_compare_fusion.6
  492.4 3.0 collective-permute-start.6
  511.0 4.6 collective-permute-done.5
  515.6 2.8 collective-permute-done.7
  525.7 2.6 select_compare_fusion.6
  546.9 4.8 collective-permute-start.7
  566.0 2.6 select_compare_fusion.6
  580.1 4.1 collective-permute-start.6
  599.8 5.3 collective-permute-done.5
  605.1 2.7 collective-permute-done.7
  615.1 2.6 select_compare_fusion.6
  644.3 5.5 collective-permute-done.5
  659.4 2.6 select_compare_fusion.6
  682.3 4.0 collective-permute-done.3
  697.2 2.6 select_compare_fusion.6
  721.1 6.1 collective-permute-start.7
  731.8 3.2 fusion.91
  737.6 70.7 %reduce-scatter.2.cloned.1.call-done = bf16[256,2048]{1,0:T(8,128)(2,1)} async-done(((bf16[256,8192]{1,0:T(8,128)(2,1)}), bf16[256,2048]{1,0:T(8,128)(2,1)}) %reduce-scatter.2.cloned.1.call-update) | async-done | bytes 1048592 | tf_op jit(solution)/shard_map/reduce_scatter | solution.py:137
  (1002 shorter events, 516.9 us)
Async XLA Ops:
  7.2 801.2 %reduce-scatter.2.cloned.1.call-start = ((), (), s32[]{:S(2)}) async-start(), calls=%async_computation.1 | async-start | bytes 5242880 | tf_op jit(solution)/shard_map/reduce_scatter | solution.py:137
  41.0 28.0 %collective-permute-start.2 = (bf16[256,1,128]{2,0,1:T(8,128)(2,1)}, bf16[256,1,128]{2,0,1:T(8,128)(2,1)}, u32[]{:S(2)}, u32[]{:S(2)}) collective-permute-start(bf16[256,1,128]{2,0,1:T(8,128)(2,1)} %get-tuple-element.745), channel_id=1, source_target_pairs={{124,0},{0,4},{4,8},{8,12},{12,16},{16,20},{20,24},{24,28},{28,32}... | collective-permute-start | bytes 196616 | tf_op jit(solution)/shard_map/while/body/eval_jaxpr/ppermute | solution.py:15
  41.4 25.5 %collective-permute-start = (bf16[256,1,128]{2,0,1:T(8,128)(2,1)S(1)}, bf16[256,1,128]{2,0,1:T(8,128)(2,1)S(1)}, u32[]{:S(2)}, u32[]{:S(2)}) collective-permute-start(bf16[256,1,128]{2,0,1:T(8,128)(2,1)S(1)} %get-tuple-element.744), channel_id=1, source_target_pairs={{124,0},{0,4},{4,8},{8,12},{12,16},{16,20},{20,24},{24,28},{28,32}... | collective-permute-start | bytes 196616 | tf_op jit(solution)/shard_map/while/body/eval_jaxpr/ppermute | solution.py:15
  82.1 26.1 %collective-permute-start.2 = (bf16[256,1,128]{2,0,1:T(8,128)(2,1)}, bf16[256,1,128]{2,0,1:T(8,128)(2,1)}, u32[]{:S(2)}, u32[]{:S(2)}) collective-permute-start(bf16[256,1,128]{2,0,1:T(8,128)(2,1)} %get-tuple-element.745), channel_id=1, source_target_pairs={{124,0},{0,4},{4,8},{8,12},{12,16},{16,20},{20,24},{24,28},{28,32}... | collective-permute-start | bytes 196616 | tf_op jit(solution)/shard_map/while/body/eval_jaxpr/ppermute | solution.py:15
  82.1 24.0 %collective-permute-start = (bf16[256,1,128]{2,0,1:T(8,128)(2,1)S(1)}, bf16[256,1,128]{2,0,1:T(8,128)(2,1)S(1)}, u32[]{:S(2)}, u32[]{:S(2)}) collective-permute-start(bf16[256,1,128]{2,0,1:T(8,128)(2,1)S(1)} %get-tuple-element.744), channel_id=1, source_target_pairs={{124,0},{0,4},{4,8},{8,12},{12,16},{16,20},{20,24},{24,28},{28,32}... | collective-permute-start | bytes 196616 | tf_op jit(solution)/shard_map/while/body/eval_jaxpr/ppermute | solution.py:15
  100.0 14.9 %collective-permute-start.4 = (f32[256,1,128]{2,0,1:T(8,128)}, f32[256,1,128]{2,0,1:T(8,128)S(1)}, u32[]{:S(2)}, u32[]{:S(2)}) collective-permute-start(f32[256,1,128]{2,0,1:T(8,128)} %maximum_add_fusion.8), channel_id=1, source_target_pairs={{124,0},{0,4},{4,8},{8,12},{12,16},{16,20},{20,24},{24,28},{28,32}... | collective-permute-start | bytes 393224 | tf_op jit(solution)/shard_map/while/body/eval_jaxpr/ppermute | solution.py:15
  101.2 13.8 %collective-permute-start.6 = (f32[256,1,128]{2,0,1:T(8,128)}, f32[256,1,128]{2,0,1:T(8,128)S(1)}, u32[]{:S(2)}, u32[]{:S(2)}) collective-permute-start(f32[256,1,128]{2,0,1:T(8,128)} %maximum_add_fusion.10), channel_id=1, source_target_pairs={{124,0},{0,4},{4,8},{8,12},{12,16},{16,20},{20,24},{24,28},{28,32}... | collective-permute-start | bytes 393224 | tf_op jit(solution)/shard_map/while/body/eval_jaxpr/ppermute | solution.py:15
  124.4 27.7 %collective-permute-start.2 = (bf16[256,1,128]{2,0,1:T(8,128)(2,1)}, bf16[256,1,128]{2,0,1:T(8,128)(2,1)}, u32[]{:S(2)}, u32[]{:S(2)}) collective-permute-start(bf16[256,1,128]{2,0,1:T(8,128)(2,1)} %get-tuple-element.745), channel_id=1, source_target_pairs={{124,0},{0,4},{4,8},{8,12},{12,16},{16,20},{20,24},{24,28},{28,32}... | collective-permute-start | bytes 196616 | tf_op jit(solution)/shard_map/while/body/eval_jaxpr/ppermute | solution.py:15
  124.4 25.6 %collective-permute-start = (bf16[256,1,128]{2,0,1:T(8,128)(2,1)S(1)}, bf16[256,1,128]{2,0,1:T(8,128)(2,1)S(1)}, u32[]{:S(2)}, u32[]{:S(2)}) collective-permute-start(bf16[256,1,128]{2,0,1:T(8,128)(2,1)S(1)} %get-tuple-element.744), channel_id=1, source_target_pairs={{124,0},{0,4},{4,8},{8,12},{12,16},{16,20},{20,24},{24,28},{28,32}... | collective-permute-start | bytes 196616 | tf_op jit(solution)/shard_map/while/body/eval_jaxpr/ppermute | solution.py:15
  167.4 26.1 %collective-permute-start.2 = (bf16[256,1,128]{2,0,1:T(8,128)(2,1)}, bf16[256,1,128]{2,0,1:T(8,128)(2,1)}, u32[]{:S(2)}, u32[]{:S(2)}) collective-permute-start(bf16[256,1,128]{2,0,1:T(8,128)(2,1)} %get-tuple-element.745), channel_id=1, source_target_pairs={{124,0},{0,4},{4,8},{8,12},{12,16},{16,20},{20,24},{24,28},{28,32}... | collective-permute-start | bytes 196616 | tf_op jit(solution)/shard_map/while/body/eval_jaxpr/ppermute | solution.py:15
  167.4 24.0 %collective-permute-start = (bf16[256,1,128]{2,0,1:T(8,128)(2,1)S(1)}, bf16[256,1,128]{2,0,1:T(8,128)(2,1)S(1)}, u32[]{:S(2)}, u32[]{:S(2)}) collective-permute-start(bf16[256,1,128]{2,0,1:T(8,128)(2,1)S(1)} %get-tuple-element.744), channel_id=1, source_target_pairs={{124,0},{0,4},{4,8},{8,12},{12,16},{16,20},{20,24},{24,28},{28,32}... | collective-permute-start | bytes 196616 | tf_op jit(solution)/shard_map/while/body/eval_jaxpr/ppermute | solution.py:15
  209.2 26.7 %collective-permute-start.2 = (bf16[256,1,128]{2,0,1:T(8,128)(2,1)}, bf16[256,1,128]{2,0,1:T(8,128)(2,1)}, u32[]{:S(2)}, u32[]{:S(2)}) collective-permute-start(bf16[256,1,128]{2,0,1:T(8,128)(2,1)} %get-tuple-element.745), channel_id=1, source_target_pairs={{124,0},{0,4},{4,8},{8,12},{12,16},{16,20},{20,24},{24,28},{28,32}... | collective-permute-start | bytes 196616 | tf_op jit(solution)/shard_map/while/body/eval_jaxpr/ppermute | solution.py:15
  209.2 24.6 %collective-permute-start = (bf16[256,1,128]{2,0,1:T(8,128)(2,1)S(1)}, bf16[256,1,128]{2,0,1:T(8,128)(2,1)S(1)}, u32[]{:S(2)}, u32[]{:S(2)}) collective-permute-start(bf16[256,1,128]{2,0,1:T(8,128)(2,1)S(1)} %get-tuple-element.744), channel_id=1, source_target_pairs={{124,0},{0,4},{4,8},{8,12},{12,16},{16,20},{20,24},{24,28},{28,32}... | collective-permute-start | bytes 196616 | tf_op jit(solution)/shard_map/while/body/eval_jaxpr/ppermute | solution.py:15
  227.1 13.3 %collective-permute-start.4 = (f32[256,1,128]{2,0,1:T(8,128)}, f32[256,1,128]{2,0,1:T(8,128)S(1)}, u32[]{:S(2)}, u32[]{:S(2)}) collective-permute-start(f32[256,1,128]{2,0,1:T(8,128)} %maximum_add_fusion.8), channel_id=1, source_target_pairs={{124,0},{0,4},{4,8},{8,12},{12,16},{16,20},{20,24},{24,28},{28,32}... | collective-permute-start | bytes 393224 | tf_op jit(solution)/shard_map/while/body/eval_jaxpr/ppermute | solution.py:15
  228.3 14.4 %collective-permute-start.6 = (f32[256,1,128]{2,0,1:T(8,128)}, f32[256,1,128]{2,0,1:T(8,128)S(1)}, u32[]{:S(2)}, u32[]{:S(2)}) collective-permute-start(f32[256,1,128]{2,0,1:T(8,128)} %maximum_add_fusion.10), channel_id=1, source_target_pairs={{124,0},{0,4},{4,8},{8,12},{12,16},{16,20},{20,24},{24,28},{28,32}... | collective-permute-start | bytes 393224 | tf_op jit(solution)/shard_map/while/body/eval_jaxpr/ppermute | solution.py:15
  251.8 29.5 %collective-permute-start.2 = (bf16[256,1,128]{2,0,1:T(8,128)(2,1)}, bf16[256,1,128]{2,0,1:T(8,128)(2,1)}, u32[]{:S(2)}, u32[]{:S(2)}) collective-permute-start(bf16[256,1,128]{2,0,1:T(8,128)(2,1)} %get-tuple-element.745), channel_id=1, source_target_pairs={{124,0},{0,4},{4,8},{8,12},{12,16},{16,20},{20,24},{24,28},{28,32}... | collective-permute-start | bytes 196616 | tf_op jit(solution)/shard_map/while/body/eval_jaxpr/ppermute | solution.py:15
  252.2 27.0 %collective-permute-start = (bf16[256,1,128]{2,0,1:T(8,128)(2,1)S(1)}, bf16[256,1,128]{2,0,1:T(8,128)(2,1)S(1)}, u32[]{:S(2)}, u32[]{:S(2)}) collective-permute-start(bf16[256,1,128]{2,0,1:T(8,128)(2,1)S(1)} %get-tuple-element.744), channel_id=1, source_target_pairs={{124,0},{0,4},{4,8},{8,12},{12,16},{16,20},{20,24},{24,28},{28,32}... | collective-permute-start | bytes 196616 | tf_op jit(solution)/shard_map/while/body/eval_jaxpr/ppermute | solution.py:15
  295.4 30.0 %collective-permute-start.2 = (bf16[256,1,128]{2,0,1:T(8,128)(2,1)}, bf16[256,1,128]{2,0,1:T(8,128)(2,1)}, u32[]{:S(2)}, u32[]{:S(2)}) collective-permute-start(bf16[256,1,128]{2,0,1:T(8,128)(2,1)} %get-tuple-element.745), channel_id=1, source_target_pairs={{124,0},{0,4},{4,8},{8,12},{12,16},{16,20},{20,24},{24,28},{28,32}... | collective-permute-start | bytes 196616 | tf_op jit(solution)/shard_map/while/body/eval_jaxpr/ppermute | solution.py:15
  295.4 27.9 %collective-permute-start = (bf16[256,1,128]{2,0,1:T(8,128)(2,1)S(1)}, bf16[256,1,128]{2,0,1:T(8,128)(2,1)S(1)}, u32[]{:S(2)}, u32[]{:S(2)}) collective-permute-start(bf16[256,1,128]{2,0,1:T(8,128)(2,1)S(1)} %get-tuple-element.744), channel_id=1, source_target_pairs={{124,0},{0,4},{4,8},{8,12},{12,16},{16,20},{20,24},{24,28},{28,32}... | collective-permute-start | bytes 196616 | tf_op jit(solution)/shard_map/while/body/eval_jaxpr/ppermute | solution.py:15
  313.3 16.6 %collective-permute-start.4 = (f32[256,1,128]{2,0,1:T(8,128)}, f32[256,1,128]{2,0,1:T(8,128)S(1)}, u32[]{:S(2)}, u32[]{:S(2)}) collective-permute-start(f32[256,1,128]{2,0,1:T(8,128)} %maximum_add_fusion.8), channel_id=1, source_target_pairs={{124,0},{0,4},{4,8},{8,12},{12,16},{16,20},{20,24},{24,28},{28,32}... | collective-permute-start | bytes 393224 | tf_op jit(solution)/shard_map/while/body/eval_jaxpr/ppermute | solution.py:15
  315.5 14.6 %collective-permute-start.6 = (f32[256,1,128]{2,0,1:T(8,128)}, f32[256,1,128]{2,0,1:T(8,128)S(1)}, u32[]{:S(2)}, u32[]{:S(2)}) collective-permute-start(f32[256,1,128]{2,0,1:T(8,128)} %maximum_add_fusion.10), channel_id=1, source_target_pairs={{124,0},{0,4},{4,8},{8,12},{12,16},{16,20},{20,24},{24,28},{28,32}... | collective-permute-start | bytes 393224 | tf_op jit(solution)/shard_map/while/body/eval_jaxpr/ppermute | solution.py:15
  342.3 27.6 %collective-permute-start.2 = (bf16[256,1,128]{2,0,1:T(8,128)(2,1)}, bf16[256,1,128]{2,0,1:T(8,128)(2,1)}, u32[]{:S(2)}, u32[]{:S(2)}) collective-permute-start(bf16[256,1,128]{2,0,1:T(8,128)(2,1)} %get-tuple-element.745), channel_id=1, source_target_pairs={{124,0},{0,4},{4,8},{8,12},{12,16},{16,20},{20,24},{24,28},{28,32}... | collective-permute-start | bytes 196616 | tf_op jit(solution)/shard_map/while/body/eval_jaxpr/ppermute | solution.py:15
  342.3 25.5 %collective-permute-start = (bf16[256,1,128]{2,0,1:T(8,128)(2,1)S(1)}, bf16[256,1,128]{2,0,1:T(8,128)(2,1)S(1)}, u32[]{:S(2)}, u32[]{:S(2)}) collective-permute-start(bf16[256,1,128]{2,0,1:T(8,128)(2,1)S(1)} %get-tuple-element.744), channel_id=1, source_target_pairs={{124,0},{0,4},{4,8},{8,12},{12,16},{16,20},{20,24},{24,28},{28,32}... | collective-permute-start | bytes 196616 | tf_op jit(solution)/shard_map/while/body/eval_jaxpr/ppermute | solution.py:15
  360.2 15.2 %collective-permute-start.4 = (f32[256,1,128]{2,0,1:T(8,128)}, f32[256,1,128]{2,0,1:T(8,128)S(1)}, u32[]{:S(2)}, u32[]{:S(2)}) collective-permute-start(f32[256,1,128]{2,0,1:T(8,128)} %maximum_add_fusion.8), channel_id=1, source_target_pairs={{124,0},{0,4},{4,8},{8,12},{12,16},{16,20},{20,24},{24,28},{28,32}... | collective-permute-start | bytes 393224 | tf_op jit(solution)/shard_map/while/body/eval_jaxpr/ppermute | solution.py:15
  361.5 14.1 %collective-permute-start.6 = (f32[256,1,128]{2,0,1:T(8,128)}, f32[256,1,128]{2,0,1:T(8,128)S(1)}, u32[]{:S(2)}, u32[]{:S(2)}) collective-permute-start(f32[256,1,128]{2,0,1:T(8,128)} %maximum_add_fusion.10), channel_id=1, source_target_pairs={{124,0},{0,4},{4,8},{8,12},{12,16},{16,20},{20,24},{24,28},{28,32}... | collective-permute-start | bytes 393224 | tf_op jit(solution)/shard_map/while/body/eval_jaxpr/ppermute | solution.py:15
  387.5 26.4 %collective-permute-start.2 = (bf16[256,1,128]{2,0,1:T(8,128)(2,1)}, bf16[256,1,128]{2,0,1:T(8,128)(2,1)}, u32[]{:S(2)}, u32[]{:S(2)}) collective-permute-start(bf16[256,1,128]{2,0,1:T(8,128)(2,1)} %get-tuple-element.745), channel_id=1, source_target_pairs={{124,0},{0,4},{4,8},{8,12},{12,16},{16,20},{20,24},{24,28},{28,32}... | collective-permute-start | bytes 196616 | tf_op jit(solution)/shard_map/while/body/eval_jaxpr/ppermute | solution.py:15
  387.5 24.3 %collective-permute-start = (bf16[256,1,128]{2,0,1:T(8,128)(2,1)S(1)}, bf16[256,1,128]{2,0,1:T(8,128)(2,1)S(1)}, u32[]{:S(2)}, u32[]{:S(2)}) collective-permute-start(bf16[256,1,128]{2,0,1:T(8,128)(2,1)S(1)} %get-tuple-element.744), channel_id=1, source_target_pairs={{124,0},{0,4},{4,8},{8,12},{12,16},{16,20},{20,24},{24,28},{28,32}... | collective-permute-start | bytes 196616 | tf_op jit(solution)/shard_map/while/body/eval_jaxpr/ppermute | solution.py:15
  427.8 29.2 %collective-permute-start.2 = (bf16[256,1,128]{2,0,1:T(8,128)(2,1)}, bf16[256,1,128]{2,0,1:T(8,128)(2,1)}, u32[]{:S(2)}, u32[]{:S(2)}) collective-permute-start(bf16[256,1,128]{2,0,1:T(8,128)(2,1)} %get-tuple-element.745), channel_id=1, source_target_pairs={{124,0},{0,4},{4,8},{8,12},{12,16},{16,20},{20,24},{24,28},{28,32}... | collective-permute-start | bytes 196616 | tf_op jit(solution)/shard_map/while/body/eval_jaxpr/ppermute | solution.py:15
  427.8 27.1 %collective-permute-start = (bf16[256,1,128]{2,0,1:T(8,128)(2,1)S(1)}, bf16[256,1,128]{2,0,1:T(8,128)(2,1)S(1)}, u32[]{:S(2)}, u32[]{:S(2)}) collective-permute-start(bf16[256,1,128]{2,0,1:T(8,128)(2,1)S(1)} %get-tuple-element.744), channel_id=1, source_target_pairs={{124,0},{0,4},{4,8},{8,12},{12,16},{16,20},{20,24},{24,28},{28,32}... | collective-permute-start | bytes 196616 | tf_op jit(solution)/shard_map/while/body/eval_jaxpr/ppermute | solution.py:15
  445.7 15.5 %collective-permute-start.4 = (f32[256,1,128]{2,0,1:T(8,128)}, f32[256,1,128]{2,0,1:T(8,128)S(1)}, u32[]{:S(2)}, u32[]{:S(2)}) collective-permute-start(f32[256,1,128]{2,0,1:T(8,128)} %maximum_add_fusion.8), channel_id=1, source_target_pairs={{124,0},{0,4},{4,8},{8,12},{12,16},{16,20},{20,24},{24,28},{28,32}... | collective-permute-start | bytes 393224 | tf_op jit(solution)/shard_map/while/body/eval_jaxpr/ppermute | solution.py:15
  447.0 14.5 %collective-permute-start.6 = (f32[256,1,128]{2,0,1:T(8,128)}, f32[256,1,128]{2,0,1:T(8,128)S(1)}, u32[]{:S(2)}, u32[]{:S(2)}) collective-permute-start(f32[256,1,128]{2,0,1:T(8,128)} %maximum_add_fusion.10), channel_id=1, source_target_pairs={{124,0},{0,4},{4,8},{8,12},{12,16},{16,20},{20,24},{24,28},{28,32}... | collective-permute-start | bytes 393224 | tf_op jit(solution)/shard_map/while/body/eval_jaxpr/ppermute | solution.py:15
  473.3 28.0 %collective-permute-start.2 = (bf16[256,1,128]{2,0,1:T(8,128)(2,1)}, bf16[256,1,128]{2,0,1:T(8,128)(2,1)}, u32[]{:S(2)}, u32[]{:S(2)}) collective-permute-start(bf16[256,1,128]{2,0,1:T(8,128)(2,1)} %get-tuple-element.745), channel_id=1, source_target_pairs={{124,0},{0,4},{4,8},{8,12},{12,16},{16,20},{20,24},{24,28},{28,32}... | collective-permute-start | bytes 196616 | tf_op jit(solution)/shard_map/while/body/eval_jaxpr/ppermute | solution.py:15
  473.3 25.9 %collective-permute-start = (bf16[256,1,128]{2,0,1:T(8,128)(2,1)S(1)}, bf16[256,1,128]{2,0,1:T(8,128)(2,1)S(1)}, u32[]{:S(2)}, u32[]{:S(2)}) collective-permute-start(bf16[256,1,128]{2,0,1:T(8,128)(2,1)S(1)} %get-tuple-element.744), channel_id=1, source_target_pairs={{124,0},{0,4},{4,8},{8,12},{12,16},{16,20},{20,24},{24,28},{28,32}... | collective-permute-start | bytes 196616 | tf_op jit(solution)/shard_map/while/body/eval_jaxpr/ppermute | solution.py:15
  491.2 15.0 %collective-permute-start.4 = (f32[256,1,128]{2,0,1:T(8,128)}, f32[256,1,128]{2,0,1:T(8,128)S(1)}, u32[]{:S(2)}, u32[]{:S(2)}) collective-permute-start(f32[256,1,128]{2,0,1:T(8,128)} %maximum_add_fusion.8), channel_id=1, source_target_pairs={{124,0},{0,4},{4,8},{8,12},{12,16},{16,20},{20,24},{24,28},{28,32}... | collective-permute-start | bytes 393224 | tf_op jit(solution)/shard_map/while/body/eval_jaxpr/ppermute | solution.py:15
  492.4 13.9 %collective-permute-start.6 = (f32[256,1,128]{2,0,1:T(8,128)}, f32[256,1,128]{2,0,1:T(8,128)S(1)}, u32[]{:S(2)}, u32[]{:S(2)}) collective-permute-start(f32[256,1,128]{2,0,1:T(8,128)} %maximum_add_fusion.10), channel_id=1, source_target_pairs={{124,0},{0,4},{4,8},{8,12},{12,16},{16,20},{20,24},{24,28},{28,32}... | collective-permute-start | bytes 393224 | tf_op jit(solution)/shard_map/while/body/eval_jaxpr/ppermute | solution.py:15
  518.4 25.1 %collective-permute-start.2 = (bf16[256,1,128]{2,0,1:T(8,128)(2,1)}, bf16[256,1,128]{2,0,1:T(8,128)(2,1)}, u32[]{:S(2)}, u32[]{:S(2)}) collective-permute-start(bf16[256,1,128]{2,0,1:T(8,128)(2,1)} %get-tuple-element.745), channel_id=1, source_target_pairs={{124,0},{0,4},{4,8},{8,12},{12,16},{16,20},{20,24},{24,28},{28,32}... | collective-permute-start | bytes 196616 | tf_op jit(solution)/shard_map/while/body/eval_jaxpr/ppermute | solution.py:15
  518.4 23.0 %collective-permute-start = (bf16[256,1,128]{2,0,1:T(8,128)(2,1)S(1)}, bf16[256,1,128]{2,0,1:T(8,128)(2,1)S(1)}, u32[]{:S(2)}, u32[]{:S(2)}) collective-permute-start(bf16[256,1,128]{2,0,1:T(8,128)(2,1)S(1)} %get-tuple-element.744), channel_id=1, source_target_pairs={{124,0},{0,4},{4,8},{8,12},{12,16},{16,20},{20,24},{24,28},{28,32}... | collective-permute-start | bytes 196616 | tf_op jit(solution)/shard_map/while/body/eval_jaxpr/ppermute | solution.py:15
  556.3 33.8 %collective-permute-start.2 = (bf16[256,1,128]{2,0,1:T(8,128)(2,1)}, bf16[256,1,128]{2,0,1:T(8,128)(2,1)}, u32[]{:S(2)}, u32[]{:S(2)}) collective-permute-start(bf16[256,1,128]{2,0,1:T(8,128)(2,1)} %get-tuple-element.745), channel_id=1, source_target_pairs={{124,0},{0,4},{4,8},{8,12},{12,16},{16,20},{20,24},{24,28},{28,32}... | collective-permute-start | bytes 196616 | tf_op jit(solution)/shard_map/while/body/eval_jaxpr/ppermute | solution.py:15
  556.7 31.3 %collective-permute-start = (bf16[256,1,128]{2,0,1:T(8,128)(2,1)S(1)}, bf16[256,1,128]{2,0,1:T(8,128)(2,1)S(1)}, u32[]{:S(2)}, u32[]{:S(2)}) collective-permute-start(bf16[256,1,128]{2,0,1:T(8,128)(2,1)S(1)} %get-tuple-element.744), channel_id=1, source_target_pairs={{124,0},{0,4},{4,8},{8,12},{12,16},{16,20},{20,24},{24,28},{28,32}... | collective-permute-start | bytes 196616 | tf_op jit(solution)/shard_map/while/body/eval_jaxpr/ppermute | solution.py:15
  576.6 18.6 %collective-permute-start.4 = (f32[256,1,128]{2,0,1:T(8,128)}, f32[256,1,128]{2,0,1:T(8,128)S(1)}, u32[]{:S(2)}, u32[]{:S(2)}) collective-permute-start(f32[256,1,128]{2,0,1:T(8,128)} %maximum_add_fusion.8), channel_id=1, source_target_pairs={{124,0},{0,4},{4,8},{8,12},{12,16},{16,20},{20,24},{24,28},{28,32}... | collective-permute-start | bytes 393224 | tf_op jit(solution)/shard_map/while/body/eval_jaxpr/ppermute | solution.py:15
  580.1 15.3 %collective-permute-start.6 = (f32[256,1,128]{2,0,1:T(8,128)}, f32[256,1,128]{2,0,1:T(8,128)S(1)}, u32[]{:S(2)}, u32[]{:S(2)}) collective-permute-start(f32[256,1,128]{2,0,1:T(8,128)} %maximum_add_fusion.10), channel_id=1, source_target_pairs={{124,0},{0,4},{4,8},{8,12},{12,16},{16,20},{20,24},{24,28},{28,32}... | collective-permute-start | bytes 393224 | tf_op jit(solution)/shard_map/while/body/eval_jaxpr/ppermute | solution.py:15
  607.8 26.8 %collective-permute-start.2 = (bf16[256,1,128]{2,0,1:T(8,128)(2,1)}, bf16[256,1,128]{2,0,1:T(8,128)(2,1)}, u32[]{:S(2)}, u32[]{:S(2)}) collective-permute-start(bf16[256,1,128]{2,0,1:T(8,128)(2,1)} %get-tuple-element.745), channel_id=1, source_target_pairs={{124,0},{0,4},{4,8},{8,12},{12,16},{16,20},{20,24},{24,28},{28,32}... | collective-permute-start | bytes 196616 | tf_op jit(solution)/shard_map/while/body/eval_jaxpr/ppermute | solution.py:15
  607.8 24.7 %collective-permute-start = (bf16[256,1,128]{2,0,1:T(8,128)(2,1)S(1)}, bf16[256,1,128]{2,0,1:T(8,128)(2,1)S(1)}, u32[]{:S(2)}, u32[]{:S(2)}) collective-permute-start(bf16[256,1,128]{2,0,1:T(8,128)(2,1)S(1)} %get-tuple-element.744), channel_id=1, source_target_pairs={{124,0},{0,4},{4,8},{8,12},{12,16},{16,20},{20,24},{24,28},{28,32}... | collective-permute-start | bytes 196616 | tf_op jit(solution)/shard_map/while/body/eval_jaxpr/ppermute | solution.py:15
  625.7 14.3 %collective-permute-start.4 = (f32[256,1,128]{2,0,1:T(8,128)}, f32[256,1,128]{2,0,1:T(8,128)S(1)}, u32[]{:S(2)}, u32[]{:S(2)}) collective-permute-start(f32[256,1,128]{2,0,1:T(8,128)} %maximum_add_fusion.8), channel_id=1, source_target_pairs={{124,0},{0,4},{4,8},{8,12},{12,16},{16,20},{20,24},{24,28},{28,32}... | collective-permute-start | bytes 393224 | tf_op jit(solution)/shard_map/while/body/eval_jaxpr/ppermute | solution.py:15
  652.1 25.1 %collective-permute-start.2 = (bf16[256,1,128]{2,0,1:T(8,128)(2,1)}, bf16[256,1,128]{2,0,1:T(8,128)(2,1)}, u32[]{:S(2)}, u32[]{:S(2)}) collective-permute-start(bf16[256,1,128]{2,0,1:T(8,128)(2,1)} %get-tuple-element.745), channel_id=1, source_target_pairs={{124,0},{0,4},{4,8},{8,12},{12,16},{16,20},{20,24},{24,28},{28,32}... | collective-permute-start | bytes 196616 | tf_op jit(solution)/shard_map/while/body/eval_jaxpr/ppermute | solution.py:15
  652.1 23.0 %collective-permute-start = (bf16[256,1,128]{2,0,1:T(8,128)(2,1)S(1)}, bf16[256,1,128]{2,0,1:T(8,128)(2,1)S(1)}, u32[]{:S(2)}, u32[]{:S(2)}) collective-permute-start(bf16[256,1,128]{2,0,1:T(8,128)(2,1)S(1)} %get-tuple-element.744), channel_id=1, source_target_pairs={{124,0},{0,4},{4,8},{8,12},{12,16},{16,20},{20,24},{24,28},{28,32}... | collective-permute-start | bytes 196616 | tf_op jit(solution)/shard_map/while/body/eval_jaxpr/ppermute | solution.py:15
  690.0 27.3 %collective-permute-start.2 = (bf16[256,1,128]{2,0,1:T(8,128)(2,1)}, bf16[256,1,128]{2,0,1:T(8,128)(2,1)}, u32[]{:S(2)}, u32[]{:S(2)}) collective-permute-start(bf16[256,1,128]{2,0,1:T(8,128)(2,1)} %get-tuple-element.745), channel_id=1, source_target_pairs={{124,0},{0,4},{4,8},{8,12},{12,16},{16,20},{20,24},{24,28},{28,32}... | collective-permute-start | bytes 196616 | tf_op jit(solution)/shard_map/while/body/eval_jaxpr/ppermute | solution.py:15
  690.0 25.2 %collective-permute-start = (bf16[256,1,128]{2,0,1:T(8,128)(2,1)S(1)}, bf16[256,1,128]{2,0,1:T(8,128)(2,1)S(1)}, u32[]{:S(2)}, u32[]{:S(2)}) collective-permute-start(bf16[256,1,128]{2,0,1:T(8,128)(2,1)S(1)} %get-tuple-element.744), channel_id=1, source_target_pairs={{124,0},{0,4},{4,8},{8,12},{12,16},{16,20},{20,24},{24,28},{28,32}... | collective-permute-start | bytes 196616 | tf_op jit(solution)/shard_map/while/body/eval_jaxpr/ppermute | solution.py:15
  (168 other events, 1691.5 us)
Sparse Core Ops, SparseCore 0:
  735.2 73.1 reduce-scatter.1
where the time goes:
time: 825 us; the launch traced here: 815 us
  matrix products  232 us (28%)
  waiting for transfers between devices  188 us (23%)
  other arithmetic  139 us (17%)
  starting transfers between devices  99.3 us (12%)
  local copies, waits for them, and re-layouts  79.9 us (10%)
  loops' own time  45.7 us (6%)
  blocking collectives  17.4 us (2%)
  between operations  14.8 us (2%)
    ppermute x128, waiting for transfers between devices, passed_along(): return lax.ppermute(block, axis, route)  117 us
    ppermute x128, starting transfers between devices, passed_along(): return lax.ppermute(block, axis, route)  99.2 us
    dot_general x64, matrix products, dense(): jnp.einsum('hgij,jhd->ihgd', score_low, span_keys, preferred_element_type...  87.7 us
    eq x32, other arithmetic, dense(): row_document[:, None] == key_document  83.1 us
    reduce_scatter x1, waiting for transfers between devices, per_device(): lax.psum_scatter(term.astype(jnp.bfloat16), 'head', scatter_dimension=1,...  70.7 us
    dot_general x64, matrix products, dense(): jnp.einsum('ihgd,jhd->hgij', grads, span_values, preferred_element_type=j...  67.6 us
    another operation x1, loops' own time, sweep(): return lax.fori_loop(0, members // 2, turn, state)  45.7 us
    dot_general x64, matrix products, dense(): jnp.einsum('ihgd,jhd->hgij', queries, span_keys, preferred_element_type=j...  35.3 us
  transfers between devices with their start and end apart: 129, of which 59 were waited for; matrix products, arithmetic and copies ran while one was open for 51% of the time, Pallas kernels for 0%

commit v1 on v0

v1 whole, which is shorter than its diff:
```python
import math

import jax
import jax.numpy as jnp
from jax import lax
from jax.experimental import pallas as pl
from jax.experimental.pallas import tpu as pltpu
from jax.sharding import PartitionSpec as P

HEAD_DIM = 128
SPAN = 128
GROUP = 8
SCALE = 1.0 / math.sqrt(HEAD_DIM)
LOG2E = math.log2(math.e)
HIDDEN = -1e30
MESH = pl.DeviceIdType.MESH
F32, BF16, I32 = jnp.float32, jnp.bfloat16, jnp.int32
NN = (((1,), (0,)), ((), ()))
NT = (((1,), (1,)), ((), ()))
PIECE = 4 * SPAN
STEPS = 5
ENTRIES = 4 * STEPS
EMPTY, DIAG_HI, DIAG_LO = ENTRIES, ENTRIES + 1, ENTRIES + 2
AROUND = (1, 3, 2)


def dot(a, b, dims=NN):
    return lax.dot_general(a, b, dims, preferred_element_type=F32)


def kernel(q, do, o, norm, k, v, order, segment, wk, wv, dq_out, dk_out, dv_out, ig_out, *scratch):
    names = [n for n, _ in SCRATCH]
    s = dict(zip(names, scratch))
    qs, ds = [s[f"qs{i}"] for i in range(4)], [s[f"ds{i}"] for i in range(4)]
    qt, dt = [s[f"qt{i}"] for i in range(4)], [s[f"dt{i}"] for i in range(4)]
    nrm, dlt = [s[f"nrm{i}"] for i in range(4)], [s[f"dlt{i}"] for i in range(4)]
    dqa = [s[f"dqa{i}"] for i in range(4)]
    nd = [s["nd0"], s["nd1"]]
    tab, tabz = s["tab"], s["tabz"]
    kbuf, vbuf, acck, accv = s["kbuf"], s["vbuf"], s["acck"], s["accv"]
    bk, bv = [s["bk0"], s["bk1"]], [s["bv0"], s["bv1"]]
    pos_lo, pos_hi, ent, vis, turn = s["pos_lo"], s["pos_hi"], s["ent"], s["vis"], s["turn"]
    kg, wg = s["kg"], s["wg"]

    ctx, head = lax.axis_index("ctx"), lax.axis_index("head")
    z, y, x = ctx // 16, (ctx // 4) % 4, ctx % 4
    me = y * 4 + x

    def at_x(d):
        return (z * 16 + y * 4 + (x + d) % 4, head)

    def at_y(d):
        return (z * 16 + ((y + d) % 4) * 4 + x, head)

    over = ((1 - z) * 16 + me, head)
    mate = head + 1 - 2 * (head % 2)
    far, far_mate = (head + 2) % 4, 3 - head
    weight_peers = ((ctx, mate), ((1 - z) * 16 + me, far), ((1 - z) * 16 + me, far_mate))
    head_peers = ((ctx, mate), (ctx, far), (ctx, far_mate))

    barrier = pltpu.get_barrier_semaphore()
    peers = [at_x(d) for d in AROUND] + [at_y(d) for d in AROUND] + [over]
    peers += [weight_peers[0], weight_peers[1], weight_peers[2], head_peers[1], head_peers[2]]
    for peer in peers:
        pl.semaphore_signal(barrier, inc=1, device_id=peer, device_id_type=MESH)

    sent = []

    def copy(src, dst, send, recv, peer):
        return pltpu.make_async_remote_copy(
            src_ref=src, dst_ref=dst, send_sem=send, recv_sem=recv, device_id=peer, device_id_type=MESH
        )

    def push(src, dst, send, recv, peer):
        c = copy(src, dst, send, recv, peer)
        c.start()
        sent.append(c)

    def arrived(dst, send, recv):
        copy(dst, dst, send, recv, over).wait_recv()

    def swapped(sel, first, second):
        shape = first.shape
        turn_round = jnp.full(shape, order[0], I32) > jnp.full(shape, order[1], I32)
        return jnp.where(turn_round, second, first) if sel == 0 else jnp.where(turn_round, first, second)

    slots = (pl.ds(0, SPAN), pl.ds(SPAN, SPAN))

    for sel in range(2):
        kbuf[2 * me + sel] = swapped(sel, k[slots[0], :], k[slots[1], :])
        vbuf[2 * me + sel] = swapped(sel, v[slots[0], :], v[slots[1], :])
    for i, value in enumerate((order[0], order[1], segment[0], segment[1])):
        tab[me, 0, i] = value

    def stack(p):
        for sel in range(2):
            for hh in range(4):
                r = pl.ds(hh * SPAN, SPAN)
                c = pl.ds((p * 4 + hh) * HEAD_DIM, HEAD_DIM)
                qs[p][sel, r, :] = swapped(sel, q[slots[0], c], q[slots[1], c])
                ds[p][sel, r, :] = swapped(sel, do[slots[0], c], do[slots[1], c])

    stack(0)
    stack(1)
    pl.semaphore_wait(barrier, len(peers))

    ks, vs = s["k_send"], s["v_send"]
    kr, vr = s["k_recv"], s["v_recv"]
    own = pl.ds(2 * me, 2)
    ms, mr, mrow = s["m_send"], s["m_recv"], s["m_row"]
    for i, d in enumerate(AROUND):
        push(tab.at[me], tab.at[me], ms.at[i], mr.at[me], at_x(d))
    for i, d in enumerate(AROUND):
        push(kbuf.at[own], kbuf.at[own], ks.at[i], kr.at[me], at_x(d))
        push(vbuf.at[own], vbuf.at[own], vs.at[i], vr.at[me], at_y(d))
    zs, zr = s["z_send"], s["z_recv"]
    push(tab.at[me], tabz.at[0], ms.at[6], s["mz_recv"].at[0], over)
    push(qs[0], qs[2], zs.at[0], zr.at[0], over)
    push(ds[0], ds[2], zs.at[1], zr.at[1], over)
    for i, d in enumerate(AROUND):
        push(kbuf.at[own], kbuf.at[own], ks.at[3 + i], kr.at[me], at_y(d))
        push(vbuf.at[own], vbuf.at[own], vs.at[3 + i], vr.at[me], at_x(d))
    ws, wr = s["w_send"], s["w_recv"]
    fill = []
    for i, w in enumerate((wk, wv)):
        columns = w.shape[0] // 4
        for j, peer in enumerate(weight_peers):
            rows = pl.ds(pl.multiple_of(peer[1] * columns, columns), columns)
            push(w.at[rows], wg.at[i, head], ws.at[3 * i + j], wr.at[4 * i + head], peer)
        rows = pl.ds(pl.multiple_of(head * columns, columns), columns)
        fill.append(pltpu.make_async_copy(w.at[rows], wg.at[i, head], s["fill"].at[i]))
        fill[-1].start()

    lane = lax.broadcasted_iota(I32, (2 * SPAN, 128), 1)
    sums = jnp.zeros((2 * SPAN, 128), F32)
    for h in range(GROUP):
        c = pl.ds(h * HEAD_DIM, HEAD_DIM)
        term = jnp.sum(do[:, c].astype(F32) * o[:, c].astype(F32), axis=1, keepdims=True)
        sums = jnp.where(lane == h, term, sums)
    sums = sums.T[0:8, :]
    for sel in range(2):
        c = pl.ds(sel * SPAN, SPAN)
        nd[0][0:8, c] = swapped(sel, norm[:, slots[0]], norm[:, slots[1]])
        nd[0][8:16, c] = swapped(sel, sums[:, :SPAN], sums[:, SPAN:])
    push(nd[0], nd[1], zs.at[2], zr.at[2], over)
    push(qs[1], qs[3], zs.at[3], zr.at[3], over)
    push(ds[1], ds[3], zs.at[4], zr.at[4], over)

    def spread(g):
        rows = jnp.concatenate([nd[g][...], jnp.zeros((112, 2 * SPAN), F32)], axis=0).T
        for p in range(2):
            for sel in range(2):
                part = rows[sel * SPAN : (sel + 1) * SPAN, :]
                for hh in range(4):
                    h, r = p * 4 + hh, pl.ds(hh * SPAN, SPAN)
                    nrm[2 * g + p][sel, r, :] = jnp.broadcast_to(part[:, h : h + 1] * LOG2E, (SPAN, 128))
                    dlt[2 * g + p][sel, r, :] = jnp.broadcast_to(part[:, 8 + h : 9 + h], (SPAN, 128))

    def turned(i):
        for sel in range(2):
            for hh in range(4):
                r = pl.ds(hh * SPAN, SPAN)
                qt[i][sel, :, r] = qs[i][sel, r, :].T
                dt[i][sel, :, r] = ds[i][sel, r, :].T

    def step(i, sel, k4, v4, bias=None, mask=None):
        n = k4.shape[0] // 128
        e = dot(qs[i][sel], k4, NT) * (SCALE * LOG2E) - jnp.concatenate([nrm[i][sel]] * n, axis=1)
        if bias is not None:
            e = e + bias
        if mask is not None:
            e = jnp.where(mask, e, HIDDEN)
        attend = jnp.exp2(e)
        grad = dot(ds[i][sel], v4, NT) - jnp.concatenate([dlt[i][sel]] * n, axis=1)
        score = (attend * grad).astype(BF16)
        return score, dot(qt[i][sel], score), dot(dt[i][sel], attend.astype(BF16))

    def bias_row(seen):
        return jnp.concatenate(
            [jnp.where(jnp.full((1, 128), one, I32) > 0, 0.0, HIDDEN) for one in seen], axis=1
        )

    def columns_of(a, u):
        return a[:, u * 128 : (u + 1) * 128]

    spread(0)
    turned(0)
    turned(1)
    row = lax.broadcasted_iota(I32, (PIECE, 128), 0) % SPAN
    below = lax.broadcasted_iota(I32, (PIECE, 128), 1) <= row
    for sel in range(2):
        k1, v1 = kbuf[2 * me + sel], vbuf[2 * me + sel]
        place = DIAG_HI if sel else DIAG_LO
        score, dk0, dv0 = step(0, sel, k1, v1, mask=below)
        dqa[0][sel] = dot(score, k1)
        score, dk1, dv1 = step(1, sel, k1, v1, mask=below)
        dqa[1][sel] = dot(score, k1)
        bk[0][place] = dk0 + dk1
        bv[0][place] = dv0 + dv1
    for g in range(2):
        bk[g][EMPTY] = jnp.zeros((128, 128), F32)
        bv[g][EMPTY] = jnp.zeros((128, 128), F32)
    for i in (2, 3):
        dqa[i][...] = jnp.zeros_like(dqa[i])

    for i, d in enumerate(AROUND):
        arrived(tab.at[y * 4 + (x + 4 - d) % 4], ms.at[0], mr.at[y * 4 + (x + 4 - d) % 4])
    for i, d in enumerate(AROUND):
        line = pl.ds(y * 4, 4)
        push(tab.at[line], tab.at[line], ms.at[3 + i], mrow.at[y], at_y(d))
    for i, d in enumerate(AROUND):
        j = y * 4 + (x + 4 - d) % 4
        two = pl.ds(2 * j, 2)
        arrived(kbuf.at[two], ks.at[0], kr.at[j])
        for n, e in enumerate(AROUND):
            push(kbuf.at[two], kbuf.at[two], ks.at[6 + 3 * i + n], kr.at[j], at_y(e))
        j = ((y + 4 - d) % 4) * 4 + x
        two = pl.ds(2 * j, 2)
        arrived(vbuf.at[two], vs.at[0], vr.at[j])
        for n, e in enumerate(AROUND):
            push(vbuf.at[two], vbuf.at[two], vs.at[6 + 3 * i + n], vr.at[j], at_x(e))

    def low_span(j):
        return jnp.minimum(tab[j, 0, 0], tab[j, 0, 1])

    def query_spans(t, j):
        first = t[j, 0, 0] < t[j, 0, 1]
        low = jnp.where(first, t[j, 0, 0], t[j, 0, 1])
        return low, jnp.where(first, t[j, 0, 2], t[j, 0, 3]), jnp.where(first, t[j, 0, 3], t[j, 0, 2])

    def later_rows(pieces, r, seg_hi, fresh):
        j0 = ((y + r) % 4) * 4
        k4 = jnp.concatenate([kbuf[2 * (j0 + u)] for u in range(4)], axis=0)
        v4 = jnp.concatenate([vbuf[2 * (j0 + u)] for u in range(4)], axis=0)
        bias = bias_row([low_span(j0 + u) - seg_hi + 1 for u in range(4)])
        dks = dvs = None
        for i in pieces:
            score, dk, dv = step(i, 1, k4, v4, bias=bias)
            dqa[i][1] += dot(score, k4)
            dks, dvs = (dk, dv) if dks is None else (dks + dk, dvs + dv)
        for u in range(4):
            if fresh:
                acck[j0 + u] = columns_of(dks, u)
                accv[j0 + u] = columns_of(dvs, u)
            else:
                acck[j0 + u] += columns_of(dks, u)
                accv[j0 + u] += columns_of(dvs, u)

    def sorted_rows(pieces, g, t, fresh):
        sel = jnp.where(t >= turn[g], 1, 0)
        k4 = jnp.concatenate([kbuf[ent[g * ENTRIES + 4 * t + u]] for u in range(4)], axis=0)
        v4 = jnp.concatenate([vbuf[ent[g * ENTRIES + 4 * t + u]] for u in range(4)], axis=0)
        bias = bias_row([vis[g * ENTRIES + 4 * t + u] for u in range(4)])
        none = jnp.zeros_like(k4)
        early = jnp.full(k4.shape, sel, I32) == 0
        wide = jnp.concatenate([jnp.where(early, k4, none), jnp.where(early, none, k4)], axis=1)
        dks = dvs = None
        for i in pieces:
            score, dk, dv = step(i, sel, k4, v4, bias=bias)
            both = dot(score, wide)
            dqa[i][0] += both[:, :128]
            dqa[i][1] += both[:, 128:]
            dks, dvs = (dk, dv) if dks is None else (dks + dk, dvs + dv)
        for u in range(4):
            if fresh:
                bk[g][4 * t + u] = columns_of(dks, u)
                bv[g][4 * t + u] = columns_of(dvs, u)
            else:
                bk[g][4 * t + u] += columns_of(dks, u)
                bv[g][4 * t + u] += columns_of(dvs, u)

    lo_own, seg_lo_own, seg_hi_own = query_spans(tab, me)

    def own_line(r, _):
        j0 = ((y + r) % 4) * 4
        for u in range(4):
            j = j0 + u
            two = pl.ds(2 * j, 2)

            @pl.when(r > 0)
            def _():
                arrived(kbuf.at[two], ks.at[0], kr.at[j])

            @pl.when(x != u)
            def _():
                arrived(vbuf.at[two], vs.at[0], vr.at[j])

        @pl.when(r > 0)
        def _():
            arrived(tab.at[pl.ds(j0, 4)], ms.at[0], mrow.at[(y + r) % 4])

        later_rows((0, 1), r, seg_hi_own, True)
        return 0

    lax.fori_loop(0, 4, own_line, 0)

    arrived(tabz.at[0], ms.at[0], s["mz_recv"].at[0])
    lo_over, seg_lo_over, seg_hi_over = query_spans(tabz, 0)
    for g, (low, seg_lo, seg_hi) in enumerate(
        ((lo_own, seg_lo_own, seg_hi_own), (lo_over, seg_lo_over, seg_hi_over))
    ):
        spans = [low_span(j) for j in range(16)]
        before = sum(jnp.where(one < low, 1, 0) for one in spans)
        upto = sum(jnp.where(one <= low, 1, 0) for one in spans)
        first = (before + 3) // 4
        turn[g] = first

        def place(j, _, g=g, low=low, spans=spans, upto=upto, first=first):
            mine = low_span(j)
            rank = sum(jnp.where(one < mine, 1, 0) for one in spans)
            hi = 4 * first + rank - upto
            pos_lo[16 * g + j] = jnp.where(mine < low, rank, jnp.where(mine == low, DIAG_LO, EMPTY))
            pos_hi[16 * g + j] = jnp.where(mine > low, hi, jnp.where(mine == low, DIAG_HI, EMPTY))
            return 0

        lax.fori_loop(0, 16, place, 0)

        def entry(p, _, g=g, spans=spans, first=first, seg_lo=seg_lo, seg_hi=seg_hi):
            index, span = jnp.int32(0), jnp.int32(-1)
            for j in range(16):
                is_lo, is_hi = pos_lo[16 * g + j] == p, pos_hi[16 * g + j] == p
                index = jnp.where(is_lo, 2 * j, jnp.where(is_hi, 2 * j + 1, index))
                span = jnp.where(is_lo, spans[j], jnp.where(is_hi, 63 - spans[j], span))
            seg = jnp.where(p < 4 * first, seg_lo, seg_hi)
            ent[g * ENTRIES + p] = index
            vis[g * ENTRIES + p] = jnp.where(span >= seg, 1, 0)
            return 0

        lax.fori_loop(0, ENTRIES, entry, 0)

    def own_sorted(t, _):
        sorted_rows((0, 1), 0, t, True)
        return 0

    lax.fori_loop(0, STEPS, own_sorted, 0)

    dqs, dqr = [s["dqs0"], s["dqs1"]], [s["dqr0"], s["dqr1"]]
    arrived(nd[1], zs.at[0], zr.at[2])
    spread(1)
    for p in range(2):
        i = 2 + p
        arrived(qs[i], zs.at[0], zr.at[3 * p])
        arrived(ds[i], zs.at[0], zr.at[3 * p + 1])
        turned(i)

        def over_line(r, _, i=i):
            later_rows((i,), r, seg_hi_over, False)
            return 0

        lax.fori_loop(0, 4, over_line, 0)

        def over_sorted(t, _, i=i, p=p):
            sorted_rows((i,), 1, t, p == 0)
            return 0

        lax.fori_loop(0, STEPS, over_sorted, 0)
        dqs[p][...] = dqa[i][...].astype(BF16)
        push(dqs[p], dqr[p], zs.at[5 + p], zr.at[5 + p], over)

    def total(acc, b, j):
        lo = acc[j] + b[0][pos_lo[j]] + b[1][pos_lo[16 + j]]
        hi = b[0][pos_hi[j]] + b[1][pos_hi[16 + j]]
        return jnp.concatenate([lo, hi], axis=1)

    sk, sv, r1k, r1v = s["sk"], s["sv"], s["r1k"], s["r1v"]
    for i, d in enumerate(AROUND):
        yd, xd = (y + d) % 4, (x + d) % 4

        def key_part(u, _, yd=yd):
            sk[yd * 4 + u] = total(acck, bk, yd * 4 + u).astype(BF16)
            return 0

        lax.fori_loop(0, 4, key_part, 0)
        push(sk.at[pl.ds(yd * 4, 4)], r1k.at[d - 1], s["s1"].at[i], s["s1r"].at[d - 1], at_y(d))

        def value_part(u, _, xd=xd):
            sv[xd * 4 + u] = total(accv, bv, u * 4 + xd).astype(BF16)
            return 0

        lax.fori_loop(0, 4, value_part, 0)
        push(sv.at[pl.ds(xd * 4, 4)], r1v.at[d - 1], s["s1"].at[3 + i], s["s1r"].at[2 + d], at_x(d))

    fk, fv, t2k, t2v, r2k, r2v = s["fk"], s["fv"], s["t2k"], s["t2v"], s["r2k"], s["r2v"]

    def own_part(u, _):
        fk[u] = total(acck, bk, y * 4 + u)
        fv[u] = total(accv, bv, u * 4 + x)
        return 0

    lax.fori_loop(0, 4, own_part, 0)
    for d in range(3):
        arrived(r1k.at[d], s["s1"].at[0], s["s1r"].at[d])

    def sum_keys(u, _):
        fk[u] += r1k[0, u].astype(F32) + r1k[1, u].astype(F32) + r1k[2, u].astype(F32)
        t2k[u] = fk[u].astype(BF16)
        return 0

    lax.fori_loop(0, 4, sum_keys, 0)
    for i, d in enumerate(AROUND):
        push(t2k.at[(x + d) % 4], r2k.at[d - 1], s["s2"].at[i], s["s2r"].at[d - 1], at_x(d))
    for d in range(3):
        arrived(r1v.at[d], s["s1"].at[0], s["s1r"].at[3 + d])

    def sum_values(u, _):
        fv[u] += r1v[0, u].astype(F32) + r1v[1, u].astype(F32) + r1v[2, u].astype(F32)
        t2v[u] = fv[u].astype(BF16)
        return 0

    lax.fori_loop(0, 4, sum_values, 0)
    for i, d in enumerate(AROUND):
        push(t2v.at[(y + d) % 4], r2v.at[d - 1], s["s2"].at[3 + i], s["s2r"].at[2 + d], at_y(d))

    for p in range(2):
        arrived(dqr[p], zs.at[0], zr.at[5 + p])
        for hh in range(4):
            r, c = pl.ds(hh * SPAN, SPAN), pl.ds((p * 4 + hh) * HEAD_DIM, HEAD_DIM)
            both = [(dqa[p][sel, r, :] + dqr[p][sel, r, :].astype(F32)) * SCALE for sel in range(2)]
            for slot in range(2):
                dq_out[slots[slot], c] = swapped(slot, both[0], both[1]).astype(BF16)

    for w, (f, r2, mine, out, scale) in enumerate(
        ((fk, r2k, x, dk_out, SCALE), (fv, r2v, y, dv_out, 1.0))
    ):
        for d in range(3):
            arrived(r2.at[d], s["s2"].at[0], s["s2r"].at[3 * w + d])
        whole = f[mine] + r2[0].astype(F32) + r2[1].astype(F32) + r2[2].astype(F32)
        both = [(columns_of(whole, sel) * scale).T for sel in range(2)]
        for slot in range(2):
            low = swapped(slot, both[0], both[1]).astype(BF16)
            out[slots[slot], :] = low
            kg[w, head, slots[slot], :] = low
        for i, peer in enumerate(head_peers):
            push(kg.at[w, head], kg.at[w, head], s["g_send"].at[3 * w + i], s["g_recv"].at[4 * w + head], peer)

    for w in range(2):
        fill[w].wait()
        for h in (mate, far, far_mate):
            arrived(wg.at[w, h], ws.at[0], wr.at[4 * w + h])
    for w in range(2):
        for h in (mate, far, far_mate):
            arrived(kg.at[w, h], ws.at[0], s["g_recv"].at[4 * w + h])

    def tile(n, _):
        cols = pl.ds(pl.multiple_of(n * 256, 256), 256)
        acc = None
        for w in range(2):
            for h in (0, 2):
                a = jnp.concatenate([kg[w, h], kg[w, h + 1]], axis=1)
                b = jnp.concatenate([wg[w, h, cols, :], wg[w, h + 1, cols, :]], axis=1)
                term = dot(a, b, NT)
                acc = term if acc is None else acc + term
        ig_out[:, cols] = acc.astype(BF16)
        return 0

    lax.fori_loop(0, ig_out.shape[1] // 256, tile, 0)
    for c in sent:
        c.wait_send()


def _scratch():
    v, dma, smem = pltpu.VMEM, pltpu.SemaphoreType.DMA, pltpu.SMEM
    out = []
    for i in range(4):
        out += [(f"qs{i}", v((2, PIECE, 128), BF16)), (f"ds{i}", v((2, PIECE, 128), BF16))]
        out += [(f"qt{i}", v((2, 128, PIECE), BF16)), (f"dt{i}", v((2, 128, PIECE), BF16))]
        out += [(f"nrm{i}", v((2, PIECE, 128), F32)), (f"dlt{i}", v((2, PIECE, 128), F32))]
        out += [(f"dqa{i}", v((2, PIECE, 128), F32))]
    for i in range(2):
        out += [(f"nd{i}", v((16, 256), F32)), (f"dqs{i}", v((2, PIECE, 128), BF16))]
        out += [(f"dqr{i}", v((2, PIECE, 128), BF16))]
        out += [(f"bk{i}", v((ENTRIES + 3, 128, 128), F32)), (f"bv{i}", v((ENTRIES + 3, 128, 128), F32))]
    out += [("tab", smem((16, 1, 128), I32)), ("tabz", smem((1, 1, 128), I32))]
    out += [("kbuf", v((32, 128, 128), BF16)), ("vbuf", v((32, 128, 128), BF16))]
    out += [("acck", v((16, 128, 128), F32)), ("accv", v((16, 128, 128), F32))]
    out += [("pos_lo", smem((32,), I32)), ("pos_hi", smem((32,), I32)), ("ent", smem((2 * ENTRIES,), I32))]
    out += [("vis", smem((2 * ENTRIES,), I32)), ("turn", smem((2,), I32))]
    out += [("sk", v((16, 128, 256), BF16)), ("sv", v((16, 128, 256), BF16))]
    for n in ("k", "v"):
        out += [(f"r1{n}", v((3, 4, 128, 256), BF16)), (f"f{n}", v((4, 128, 256), F32))]
        out += [(f"t2{n}", v((4, 128, 256), BF16)), (f"r2{n}", v((3, 128, 256), BF16))]
    out += [("kg", v((2, 4, 256, 128), BF16))]
    out += [("wg", v((2, 4, 2048, 128), BF16))]
    out += [("k_send", dma((15,))), ("v_send", dma((15,))), ("k_recv", dma((16,))), ("v_recv", dma((16,)))]
    out += [("m_send", dma((7,))), ("m_recv", dma((16,))), ("m_row", dma((4,))), ("mz_recv", dma((1,)))]
    out += [("z_send", dma((7,))), ("z_recv", dma((7,))), ("w_send", dma((6,))), ("w_recv", dma((8,)))]
    out += [("fill", dma((2,))), ("s1", dma((6,))), ("s1r", dma((6,))), ("s2", dma((6,))), ("s2r", dma((6,)))]
    out += [("g_send", dma((6,))), ("g_recv", dma((8,)))]
    return out


SCRATCH = _scratch()


def per_device(
    query, key, value, attention_out, out_grad, log_norm, span_order, span_segment, key_weight, value_weight
):
    rows = query.shape[0]
    vmem, smem = pl.BlockSpec(memory_space=pltpu.VMEM), pl.BlockSpec(memory_space=pltpu.SMEM)
    hbm = pl.BlockSpec(memory_space=pl.ANY)
    return pl.pallas_call(
        kernel,
        name="attention_backward",
        out_shape=(
            jax.ShapeDtypeStruct(query.shape, BF16),
            jax.ShapeDtypeStruct(key.shape, BF16),
            jax.ShapeDtypeStruct(value.shape, BF16),
            jax.ShapeDtypeStruct((rows, key_weight.shape[0] // 4), BF16),
        ),
        in_specs=[vmem] * 6 + [smem] * 2 + [hbm] * 2,
        out_specs=(vmem,) * 4,
        scratch_shapes=[shape for _, shape in SCRATCH],
        compiler_params=pltpu.CompilerParams(
            collective_id=0, has_side_effects=True, vmem_limit_bytes=60 << 20
        ),
        cost_estimate=pl.CostEstimate(flops=12_000_000_000, bytes_accessed=16 << 20, transcendentals=0),
    )(
        query, out_grad, attention_out, log_norm.T, key, value,
        span_order, span_segment, key_weight, value_weight,
    )


def solution(mesh):
    split = P("ctx", "head")
    in_specs = (split,) * 6 + (P("ctx"), P("ctx"), P(None, "head"), P(None, "head"))
    return jax.shard_map(
        per_device, mesh=mesh, in_specs=in_specs, out_specs=(split,) * 4, check_vma=False
    )
```

time: 825 us -> 91.9 us (0.11); the launches traced: 815 us -> 91.6 us
  matrix products: 232 us -> 0 us
  waiting for transfers between devices: 188 us -> 0 us
  other arithmetic: 139 us -> 0 us
  starting transfers between devices: 99.3 us -> 0 us
  Pallas kernels: 0 us -> 83.8 us
  local copies, waits for them, and re-layouts: 79.9 us -> 7.12 us
  loops' own time: 45.7 us -> 0 us
  blocking collectives: 17.4 us -> 0 us
  between operations: 14.8 us -> 0.64 us
    dot_general x322 -> x0, matrix products: 232 us -> none  [the longest x64 87.7 us: dense(): jnp.einsum('hgij,jhd->ihgd', score_low, span_keys, preferred_element_type...]
    ppermute x128 -> x0, waiting for transfers between devices: 117 us -> none  [passed_along(): return lax.ppermute(block, axis, route)]
    ppermute x128 -> x0, starting transfers between devices: 99.2 us -> none  [passed_along(): return lax.ppermute(block, axis, route)]
    pallas_call x0 -> x1, Pallas kernels: none -> 83.8 us  [per_device(): pl.pallas_call(kernel, name='attention_backward', out_shape=(jax.ShapeDty...]
    eq x32 -> x0, other arithmetic: 83.1 us -> none  [dense(): row_document[:, None] == key_document]
    reduce_scatter x1 -> x0, waiting for transfers between devices: 70.7 us -> none  [per_device(): lax.psum_scatter(term.astype(jnp.bfloat16), 'head', scatter_dimension=1,...]
    another operation x1 -> x0, loops' own time: 45.7 us -> none  [sweep(): return lax.fori_loop(0, members // 2, turn, state)]
    add x144 -> x0, other arithmetic: 42.1 us -> none  [the longest x16 19.8 us: per_device(): jnp.where(first_half, span_order[0], span_order[1]) * span + offsets % span]
  transfers between devices with their start and end apart: 129 -> 0, of which waited for: 59 -> 0; matrix products, arithmetic and copies ran while one was open for 51% -> 0% of each run, Pallas kernels for 0% -> 0%
where the time goes in v1:
time: 91.9 us; the launch traced here: 91.6 us
  Pallas kernels  83.8 us (91%)
  local copies, waits for them, and re-layouts  7.12 us (8%)
    pallas_call x1, Pallas kernels, per_device(): pl.pallas_call(kernel, name='attention_backward', out_shape=(jax.ShapeDty...  83.8 us
    unnamed x4, local copies, waits for them, and re-layouts  7.12 us

profile of v1, /device:TPU:1, one launch (start us, length us, event | category | flops | bytes accessed | tf_op | source)
XLA Modules:
  0.0 91.6 jit_solution(8654509310543191471)
XLA Ops:
  0.6 83.8 %attention_backward.1 = (bf16[256,1024]{1,0:T(8,128)(2,1)}, bf16[256,128]{1,0:T(8,128)(2,1)}, bf16[256,128]{1,0:T(8,128)(2,1)}, bf16[256,2048]{1,0:T(8,128)(2,1)}) custom-call(bf16[256,1024]{1,0:T(8,128)(2,1)} %q.1, bf16[256,1024]{1,0:T(8,128)(2,1)} %do.1, bf16[256,1024]{1,0:T(8,128)(2,1)} %o.1, f32[8,256]{1,0:T(8,128)} %bitcast.1, bf16[256,128]{1,0:T(8,128)(2,1)} %k.1, ...), custom_call_target="tpu_custom_call" | custom-call | flops 12000000000 | bytes 16777216 | tf_op jit(solution)/shard_map/attention_backward/pallas_call | solution.py:501
  84.5 1.9 %copy.18 = bf16[256,1024]{1,0:T(8,128)(2,1)} copy(bf16[256,1024]{1,0:T(8,128)(2,1)} %get-tuple-element.8) | data formatting | bytes 1048576
  86.4 1.5 %copy.19 = bf16[256,128]{1,0:T(8,128)(2,1)} copy(bf16[256,128]{1,0:T(8,128)(2,1)} %get-tuple-element.9) | data formatting | bytes 131072
  87.8 1.5 %copy.20 = bf16[256,128]{1,0:T(8,128)(2,1)} copy(bf16[256,128]{1,0:T(8,128)(2,1)} %get-tuple-element.10) | data formatting | bytes 131072
  89.3 2.3 %copy.21 = bf16[256,2048]{1,0:T(8,128)(2,1)} copy(bf16[256,2048]{1,0:T(8,128)(2,1)} %get-tuple-element.11) | data formatting | bytes 2097152

commit v2 on v1

--- a/solution.py
+++ b/solution.py
@@ -28,7 +28,7 @@
     return lax.dot_general(a, b, dims, preferred_element_type=F32)
 
 
-def kernel(q, do, o, norm, k, v, order, segment, wk, wv, dq_out, dk_out, dv_out, ig_out, *scratch):
+def kernel(q, do, o, norm, k, v, order, segment, wk, wv, dq_out, dk_out, dv_out, kg, wg, *scratch):
     names = [n for n, _ in SCRATCH]
     s = dict(zip(names, scratch))
     qs, ds = [s[f"qs{i}"] for i in range(4)], [s[f"ds{i}"] for i in range(4)]
@@ -40,7 +40,6 @@
     kbuf, vbuf, acck, accv = s["kbuf"], s["vbuf"], s["acck"], s["accv"]
     bk, bv = [s["bk0"], s["bk1"]], [s["bv0"], s["bv1"]]
     pos_lo, pos_hi, ent, vis, turn = s["pos_lo"], s["pos_hi"], s["ent"], s["vis"], s["turn"]
-    kg, wg = s["kg"], s["wg"]
 
     ctx, head = lax.axis_index("ctx"), lax.axis_index("head")
     z, y, x = ctx // 16, (ctx // 4) % 4, ctx % 4
@@ -186,6 +185,23 @@
     spread(0)
     turned(0)
     turned(1)
+    for i, d in enumerate(AROUND):
+        arrived(tab.at[y * 4 + (x + 4 - d) % 4], ms.at[0], mr.at[y * 4 + (x + 4 - d) % 4])
+    for i, d in enumerate(AROUND):
+        line = pl.ds(y * 4, 4)
+        push(tab.at[line], tab.at[line], ms.at[3 + i], mrow.at[y], at_y(d))
+    for i, d in enumerate(AROUND):
+        j = y * 4 + (x + 4 - d) % 4
+        two = pl.ds(2 * j, 2)
+        arrived(kbuf.at[two], ks.at[0], kr.at[j])
+        for n, e in enumerate(AROUND):
+            push(kbuf.at[two], kbuf.at[two], ks.at[6 + 3 * i + n], kr.at[j], at_y(e))
+        j = ((y + 4 - d) % 4) * 4 + x
+        two = pl.ds(2 * j, 2)
+        arrived(vbuf.at[two], vs.at[0], vr.at[j])
+        for n, e in enumerate(AROUND):
+            push(vbuf.at[two], vbuf.at[two], vs.at[6 + 3 * i + n], vr.at[j], at_x(e))
+
     row = lax.broadcasted_iota(I32, (PIECE, 128), 0) % SPAN
     below = lax.broadcasted_iota(I32, (PIECE, 128), 1) <= row
     for sel in range(2):
@@ -202,23 +218,6 @@
         bv[g][EMPTY] = jnp.zeros((128, 128), F32)
     for i in (2, 3):
         dqa[i][...] = jnp.zeros_like(dqa[i])
-
-    for i, d in enumerate(AROUND):
-        arrived(tab.at[y * 4 + (x + 4 - d) % 4], ms.at[0], mr.at[y * 4 + (x + 4 - d) % 4])
-    for i, d in enumerate(AROUND):
-        line = pl.ds(y * 4, 4)
-        push(tab.at[line], tab.at[line], ms.at[3 + i], mrow.at[y], at_y(d))
-    for i, d in enumerate(AROUND):
-        j = y * 4 + (x + 4 - d) % 4
-        two = pl.ds(2 * j, 2)
-        arrived(kbuf.at[two], ks.at[0], kr.at[j])
-        for n, e in enumerate(AROUND):
-            push(kbuf.at[two], kbuf.at[two], ks.at[6 + 3 * i + n], kr.at[j], at_y(e))
-        j = ((y + 4 - d) % 4) * 4 + x
-        two = pl.ds(2 * j, 2)
-        arrived(vbuf.at[two], vs.at[0], vr.at[j])
-        for n, e in enumerate(AROUND):
-            push(vbuf.at[two], vbuf.at[two], vs.at[6 + 3 * i + n], vr.at[j], at_x(e))
 
     def low_span(j):
         return jnp.minimum(tab[j, 0, 0], tab[j, 0, 1])
@@ -270,30 +269,8 @@
                 bv[g][4 * t + u] += columns_of(dvs, u)
 
     lo_own, seg_lo_own, seg_hi_own = query_spans(tab, me)
-
-    def own_line(r, _):
-        j0 = ((y + r) % 4) * 4
-        for u in range(4):
-            j = j0 + u
-            two = pl.ds(2 * j, 2)
-
-            @pl.when(r > 0)
-            def _():
-                arrived(kbuf.at[two], ks.at[0], kr.at[j])
-
-            @pl.when(x != u)
-            def _():
-                arrived(vbuf.at[two], vs.at[0], vr.at[j])
-
-        @pl.when(r > 0)
-        def _():
-            arrived(tab.at[pl.ds(j0, 4)], ms.at[0], mrow.at[(y + r) % 4])
-
-        later_rows((0, 1), r, seg_hi_own, True)
-        return 0
-
-    lax.fori_loop(0, 4, own_line, 0)
-
+    for r in range(1, 4):
+        arrived(tab.at[pl.ds(((y + r) % 4) * 4, 4)], ms.at[0], mrow.at[(y + r) % 4])
     arrived(tabz.at[0], ms.at[0], s["mz_recv"].at[0])
     lo_over, seg_lo_over, seg_hi_over = query_spans(tabz, 0)
     for g, (low, seg_lo, seg_hi) in enumerate(
@@ -328,6 +305,25 @@
 
         lax.fori_loop(0, ENTRIES, entry, 0)
 
+    def own_line(r, _):
+        j0 = ((y + r) % 4) * 4
+        for u in range(4):
+            j = j0 + u
+            two = pl.ds(2 * j, 2)
+
+            @pl.when(r > 0)
+            def _():
+                arrived(kbuf.at[two], ks.at[0], kr.at[j])
+
+            @pl.when(x != u)
+            def _():
+                arrived(vbuf.at[two], vs.at[0], vr.at[j])
+
+        later_rows((0, 1), r, seg_hi_own, True)
+        return 0
+
+    lax.fori_loop(0, 4, own_line, 0)
+
     def own_sorted(t, _):
         sorted_rows((0, 1), 0, t, True)
         return 0
@@ -343,73 +339,78 @@
         arrived(ds[i], zs.at[0], zr.at[3 * p + 1])
         turned(i)
 
-        def over_line(r, _, i=i):
-            later_rows((i,), r, seg_hi_over, False)
-            return 0
-
-        lax.fori_loop(0, 4, over_line, 0)
-
         def over_sorted(t, _, i=i, p=p):
             sorted_rows((i,), 1, t, p == 0)
             return 0
 
         lax.fori_loop(0, STEPS, over_sorted, 0)
-        dqs[p][...] = dqa[i][...].astype(BF16)
-        push(dqs[p], dqr[p], zs.at[5 + p], zr.at[5 + p], over)
 
     def total(acc, b, j):
         lo = acc[j] + b[0][pos_lo[j]] + b[1][pos_lo[16 + j]]
         hi = b[0][pos_hi[j]] + b[1][pos_hi[16 + j]]
-        return jnp.concatenate([lo, hi], axis=1)
+        return jnp.concatenate([lo, hi], axis=1).astype(BF16)
 
     sk, sv, r1k, r1v = s["sk"], s["sv"], s["r1k"], s["r1v"]
-    for i, d in enumerate(AROUND):
-        yd, xd = (y + d) % 4, (x + d) % 4
-
-        def key_part(u, _, yd=yd):
-            sk[yd * 4 + u] = total(acck, bk, yd * 4 + u).astype(BF16)
-            return 0
-
-        lax.fori_loop(0, 4, key_part, 0)
-        push(sk.at[pl.ds(yd * 4, 4)], r1k.at[d - 1], s["s1"].at[i], s["s1r"].at[d - 1], at_y(d))
-
-        def value_part(u, _, xd=xd):
-            sv[xd * 4 + u] = total(accv, bv, u * 4 + xd).astype(BF16)
-            return 0
-
-        lax.fori_loop(0, 4, value_part, 0)
-        push(sv.at[pl.ds(xd * 4, 4)], r1v.at[d - 1], s["s1"].at[3 + i], s["s1r"].at[2 + d], at_x(d))
-
-    fk, fv, t2k, t2v, r2k, r2v = s["fk"], s["fv"], s["t2k"], s["t2v"], s["r2k"], s["r2v"]
-
-    def own_part(u, _):
-        fk[u] = total(acck, bk, y * 4 + u)
-        fv[u] = total(accv, bv, u * 4 + x)
+    s1k, s1v, s1kr, s1vr = s["s1k"], s["s1v"], s["s1kr"], s["s1vr"]
+
+    def key_copy(d):
+        yd = (y + d) % 4
+        return copy(sk.at[pl.ds(yd * 4, 4)], r1k.at[d - 1], s1k.at[d - 1], s1kr.at[d - 1], at_y(d))
+
+    def value_copy(d, line):
+        n = (d - 1) * 4 + line
+        return copy(sv.at[(x + d) % 4 * 4 + line], r1v.at[d - 1, line], s1v.at[n], s1vr.at[n], at_x(d))
+
+    def over_line(r, _):
+        line = (y + r + 1) % 4
+        later_rows((2, 3), r + 1, seg_hi_over, False)
+        for u in range(4):
+            sk[line * 4 + u] = total(acck, bk, line * 4 + u)
+            sv[u * 4 + line] = total(accv, bv, line * 4 + u)
+
+        @pl.when(r < 3)
+        def _():
+            key_copy(r + 1).start()
+
+        for d in AROUND:
+            value_copy(d, line).start()
         return 0
 
-    lax.fori_loop(0, 4, own_part, 0)
-    for d in range(3):
-        arrived(r1k.at[d], s["s1"].at[0], s["s1r"].at[d])
+    lax.fori_loop(0, 4, over_line, 0)
+    for p in range(2):
+        dqs[p][...] = dqa[2 + p][...].astype(BF16)
+        push(dqs[p], dqr[p], zs.at[5 + p], zr.at[5 + p], over)
+
+    t2k, t2v, r2k, r2v = s["t2k"], s["t2v"], s["r2k"], s["r2v"]
+    for d in (1, 2, 3):
+        key_copy(d).wait_recv()
 
     def sum_keys(u, _):
-        fk[u] += r1k[0, u].astype(F32) + r1k[1, u].astype(F32) + r1k[2, u].astype(F32)
-        t2k[u] = fk[u].astype(BF16)
+        parts = sk[y * 4 + u].astype(F32) + r1k[0, u].astype(F32)
+        t2k[u] = (parts + r1k[1, u].astype(F32) + r1k[2, u].astype(F32)).astype(BF16)
         return 0
 
     lax.fori_loop(0, 4, sum_keys, 0)
     for i, d in enumerate(AROUND):
         push(t2k.at[(x + d) % 4], r2k.at[d - 1], s["s2"].at[i], s["s2r"].at[d - 1], at_x(d))
-    for d in range(3):
-        arrived(r1v.at[d], s["s1"].at[0], s["s1r"].at[3 + d])
-
-    def sum_values(u, _):
-        fv[u] += r1v[0, u].astype(F32) + r1v[1, u].astype(F32) + r1v[2, u].astype(F32)
-        t2v[u] = fv[u].astype(BF16)
+
+    def value_back(d):
+        return copy(t2v.at[(y + d) % 4], r2v.at[d - 1], s["s2"].at[2 + d], s["s2r"].at[2 + d], at_y(d))
+
+    def sum_values(r, _):
+        line = (y + r + 1) % 4
+        for d in AROUND:
+            value_copy(d, line).wait_recv()
+        parts = sv[x * 4 + line].astype(F32) + r1v[0, line].astype(F32)
+        t2v[line] = (parts + r1v[1, line].astype(F32) + r1v[2, line].astype(F32)).astype(BF16)
+
+        @pl.when(r < 3)
+        def _():
+            value_back(r + 1).start()
+
         return 0
 
     lax.fori_loop(0, 4, sum_values, 0)
-    for i, d in enumerate(AROUND):
-        push(t2v.at[(y + d) % 4], r2v.at[d - 1], s["s2"].at[3 + i], s["s2r"].at[2 + d], at_y(d))
 
     for p in range(2):
         arrived(dqr[p], zs.at[0], zr.at[5 + p])
@@ -419,43 +420,74 @@
             for slot in range(2):
                 dq_out[slots[slot], c] = swapped(slot, both[0], both[1]).astype(BF16)
 
-    for w, (f, r2, mine, out, scale) in enumerate(
-        ((fk, r2k, x, dk_out, SCALE), (fv, r2v, y, dv_out, 1.0))
+    fin = s["fin"]
+    for w, (t2, r2, mine, out, scale) in enumerate(
+        ((t2k, r2k, x, dk_out, SCALE), (t2v, r2v, y, dv_out, 1.0))
     ):
         for d in range(3):
             arrived(r2.at[d], s["s2"].at[0], s["s2r"].at[3 * w + d])
-        whole = f[mine] + r2[0].astype(F32) + r2[1].astype(F32) + r2[2].astype(F32)
+        whole = t2[mine].astype(F32) + r2[0].astype(F32) + r2[1].astype(F32) + r2[2].astype(F32)
         both = [(columns_of(whole, sel) * scale).T for sel in range(2)]
         for slot in range(2):
             low = swapped(slot, both[0], both[1]).astype(BF16)
             out[slots[slot], :] = low
-            kg[w, head, slots[slot], :] = low
+            fin[w, slots[slot], :] = low
+        fill.append(pltpu.make_async_copy(fin.at[w], kg.at[w, head], s["fill"].at[2 + w]))
+        fill[-1].start()
         for i, peer in enumerate(head_peers):
-            push(kg.at[w, head], kg.at[w, head], s["g_send"].at[3 * w + i], s["g_recv"].at[4 * w + head], peer)
+            push(fin.at[w], kg.at[w, head], s["g_send"].at[3 * w + i], s["g_recv"].at[4 * w + head], peer)
 
     for w in range(2):
-        fill[w].wait()
         for h in (mate, far, far_mate):
             arrived(wg.at[w, h], ws.at[0], wr.at[4 * w + h])
-    for w in range(2):
-        for h in (mate, far, far_mate):
             arrived(kg.at[w, h], ws.at[0], s["g_recv"].at[4 * w + h])
-
-    def tile(n, _):
-        cols = pl.ds(pl.multiple_of(n * 256, 256), 256)
+    for c in fill:
+        c.wait()
+    for c in sent:
+        c.wait_send()
+    for d in (1, 2, 3):
+        key_copy(d).wait_send()
+        value_back(d).wait_send()
+        for line in range(4):
+            value_copy(d, line).wait_send()
+
+
+TILES = 8
+
+
+def finish(dq, dk, dv, kg, wg, dq_out, dk_out, dv_out, ig_out, a, b, c, dq_in, dk_in, dv_in, into, out, through):
+    handed = ((dq, dq_in, dq_out), (dk, dk_in, dk_out), (dv, dv_in, dv_out))
+    inward = [pltpu.make_async_copy(src, via, through.at[i]) for i, (src, via, _) in enumerate(handed)]
+    onward = [pltpu.make_async_copy(via, dst, through.at[3 + i]) for i, (_, via, dst) in enumerate(handed)]
+    first = pltpu.make_async_copy(kg, a, into.at[TILES])
+    first.start()
+    cols = b.shape[2] // TILES
+    loads = [
+        pltpu.make_async_copy(wg.at[:, :, pl.ds(n * cols, cols)], b.at[:, :, pl.ds(n * cols, cols)], into.at[n])
+        for n in range(TILES)
+    ]
+    for one in loads + inward:
+        one.start()
+    first.wait()
+    stores = []
+    for n in range(TILES):
+        loads[n].wait()
+        r = pl.ds(n * cols, cols)
         acc = None
         for w in range(2):
             for h in (0, 2):
-                a = jnp.concatenate([kg[w, h], kg[w, h + 1]], axis=1)
-                b = jnp.concatenate([wg[w, h, cols, :], wg[w, h + 1, cols, :]], axis=1)
-                term = dot(a, b, NT)
+                left = jnp.concatenate([a[w, h], a[w, h + 1]], axis=1)
+                right = jnp.concatenate([b[w, h, r, :], b[w, h + 1, r, :]], axis=1)
+                term = dot(left, right, NT)
                 acc = term if acc is None else acc + term
-        ig_out[:, cols] = acc.astype(BF16)
-        return 0
-
-    lax.fori_loop(0, ig_out.shape[1] // 256, tile, 0)
-    for c in sent:
-        c.wait_send()
+        c[:, r] = acc.astype(BF16)
+        stores.append(pltpu.make_async_copy(c.at[:, r], ig_out.at[:, r], out.at[n]))
+        stores[-1].start()
+        if n < 3:
+            inward[n].wait()
+            onward[n].start()
+    for one in stores + onward:
+        one.wait()
 
 
 def _scratch():
@@ -477,14 +509,14 @@
     out += [("vis", smem((2 * ENTRIES,), I32)), ("turn", smem((2,), I32))]
     out += [("sk", v((16, 128, 256), BF16)), ("sv", v((16, 128, 256), BF16))]
     for n in ("k", "v"):
-        out += [(f"r1{n}", v((3, 4, 128, 256), BF16)), (f"f{n}", v((4, 128, 256), F32))]
+        out += [(f"r1{n}", v((3, 4, 128, 256), BF16))]
         out += [(f"t2{n}", v((4, 128, 256), BF16)), (f"r2{n}", v((3, 128, 256), BF16))]
-    out += [("kg", v((2, 4, 256, 128), BF16))]
-    out += [("wg", v((2, 4, 2048, 128), BF16))]
+    out += [("fin", v((2, 256, 128), BF16))]
     out += [("k_send", dma((15,))), ("v_send", dma((15,))), ("k_recv", dma((16,))), ("v_recv", dma((16,)))]
     out += [("m_send", dma((7,))), ("m_recv", dma((16,))), ("m_row", dma((4,))), ("mz_recv", dma((1,)))]
     out += [("z_send", dma((7,))), ("z_recv", dma((7,))), ("w_send", dma((6,))), ("w_recv", dma((8,)))]
-    out += [("fill", dma((2,))), ("s1", dma((6,))), ("s1r", dma((6,))), ("s2", dma((6,))), ("s2r", dma((6,)))]
+    out += [("fill", dma((4,))), ("s1k", dma((3,))), ("s1kr", dma((3,))), ("s1v", dma((12,))), ("s1vr", dma((12,)))]
+    out += [("s2", dma((6,))), ("s2r", dma((6,)))]
     out += [("g_send", dma((6,))), ("g_recv", dma((8,)))]
     return out
 
@@ -498,26 +530,52 @@
     rows = query.shape[0]
     vmem, smem = pl.BlockSpec(memory_space=pltpu.VMEM), pl.BlockSpec(memory_space=pltpu.SMEM)
     hbm = pl.BlockSpec(memory_space=pl.ANY)
-    return pl.pallas_call(
+    columns = key_weight.shape[0] // 4
+    small = (
+        jax.ShapeDtypeStruct(query.shape, BF16),
+        jax.ShapeDtypeStruct(key.shape, BF16),
+        jax.ShapeDtypeStruct(value.shape, BF16),
+    )
+    held = pl.pallas_call(
         kernel,
         name="attention_backward",
-        out_shape=(
-            jax.ShapeDtypeStruct(query.shape, BF16),
-            jax.ShapeDtypeStruct(key.shape, BF16),
-            jax.ShapeDtypeStruct(value.shape, BF16),
-            jax.ShapeDtypeStruct((rows, key_weight.shape[0] // 4), BF16),
+        out_shape=small
+        + (
+            jax.ShapeDtypeStruct((2, 4, rows, HEAD_DIM), BF16),
+            jax.ShapeDtypeStruct((2, 4, columns, HEAD_DIM), BF16),
         ),
         in_specs=[vmem] * 6 + [smem] * 2 + [hbm] * 2,
-        out_specs=(vmem,) * 4,
+        out_specs=(vmem,) * 3 + (hbm,) * 2,
         scratch_shapes=[shape for _, shape in SCRATCH],
         compiler_params=pltpu.CompilerParams(
             collective_id=0, has_side_effects=True, vmem_limit_bytes=60 << 20
         ),
-        cost_estimate=pl.CostEstimate(flops=12_000_000_000, bytes_accessed=16 << 20, transcendentals=0),
+        cost_estimate=pl.CostEstimate(flops=11_000_000_000, bytes_accessed=16 << 20, transcendentals=0),
     )(
         query, out_grad, attention_out, log_norm.T, key, value,
         span_order, span_segment, key_weight, value_weight,
     )
+    dma = pltpu.SemaphoreType.DMA
+    return pl.pallas_call(
+        finish,
+        name="input_gradient",
+        out_shape=small + (jax.ShapeDtypeStruct((rows, columns), BF16),),
+        in_specs=[hbm] * 5,
+        out_specs=(hbm,) * 4,
+        scratch_shapes=[
+            pltpu.VMEM((2, 4, rows, HEAD_DIM), BF16),
+            pltpu.VMEM((2, 4, columns, HEAD_DIM), BF16),
+            pltpu.VMEM((rows, columns), BF16),
+            pltpu.VMEM(query.shape, BF16),
+            pltpu.VMEM(key.shape, BF16),
+            pltpu.VMEM(value.shape, BF16),
+            dma((TILES + 1,)),
+            dma((TILES,)),
+            dma((6,)),
+        ],
+        compiler_params=pltpu.CompilerParams(vmem_limit_bytes=60 << 20),
+        cost_estimate=pl.CostEstimate(flops=1_100_000_000, bytes_accessed=8 << 20, transcendentals=0),
+    )(*held)
 
 
 def solution(mesh):

time: 91.9 us -> 81.3 us (0.88)
  local copies, waits for them, and re-layouts: 7.12 us -> 0 us
  Pallas kernels: 83.8 us -> 79.8 us
    unnamed x4 -> x0, local copies, waits for them, and re-layouts: 7.12 us -> none
    pallas_call x1 -> x2, Pallas kernels: 83.8 us -> 79.8 us  [the longest x1 73.6 us: per_device(): pl.pallas_call(kernel, name='attention_backward', out_shape=small + (jax....]
where the time goes in v2:
time: 81.3 us; the launch traced here: 80.6 us
  Pallas kernels  79.8 us (98%)
    pallas_call x1, Pallas kernels, per_device(): pl.pallas_call(kernel, name='attention_backward', out_shape=small + (jax....  73.6 us
    pallas_call x1, Pallas kernels, per_device(): pl.pallas_call(finish, name='input_gradient', out_shape=small + (jax.Shap...  6.19 us

profile of v2, /device:TPU:1, one launch (start us, length us, event | category | flops | bytes accessed | tf_op | source)
XLA Modules:
  0.0 80.6 jit_solution(13722257857199336302)
XLA Ops:
  0.6 73.6 %attention_backward.1 = (bf16[256,1024]{1,0:T(8,128)(2,1)}, bf16[256,128]{1,0:T(8,128)(2,1)}, bf16[256,128]{1,0:T(8,128)(2,1)}, bf16[2,4,256,128]{3,2,1,0:T(8,128)(2,1)}, bf16[2,4,2048,128]{3,2,1,0:T(8,128)(2,1)}) custom-call(bf16[256,1024]{1,0:T(8,128)(2,1)} %q.1, bf16[256,1024]{1,0:T(8,128)(2,1)} %do.1, bf16[256,1024]{1,0:T(8,128)(2,1)} %o.1, ...), custom_call_target="tpu_custom_call" | custom-call | flops 11000000512 | bytes 16777216 | tf_op jit(solution)/shard_map/attention_backward/pallas_call | solution.py:539
  74.2 6.2 %input_gradient.1 = (bf16[256,1024]{1,0:T(8,128)(2,1)}, bf16[256,128]{1,0:T(8,128)(2,1)}, bf16[256,128]{1,0:T(8,128)(2,1)}, bf16[256,2048]{1,0:T(8,128)(2,1)}) custom-call(bf16[256,1024]{1,0:T(8,128)(2,1)} %get-tuple-element.9.dq, bf16[256,128]{1,0:T(8,128)(2,1)} %get-tuple-element.10.dk, bf16[256,128]{1,0:T(8,128)(2,1)} %get-tuple-element.11.dv, ...), custom_call_target="tpu_custom_call" | custom-call | flops 1100000000 | bytes 8388608 | tf_op jit(solution)/shard_map/input_gradient/pallas_call | solution.py:559

commit v3 on v2

v3 whole, which is shorter than its diff:
```python
import math

import jax
import jax.numpy as jnp
from jax import lax
from jax.experimental import pallas as pl
from jax.experimental.pallas import tpu as pltpu
from jax.sharding import PartitionSpec as P

HEAD_DIM = 128
SPAN = 128
GROUP = 8
SCALE = 1.0 / math.sqrt(HEAD_DIM)
LOG2E = math.log2(math.e)
HIDDEN = -1e30
MESH = pl.DeviceIdType.MESH
F32, BF16, I32 = jnp.float32, jnp.bfloat16, jnp.int32
NN = (((1,), (0,)), ((), ()))
NT = (((1,), (1,)), ((), ()))
PIECE = 4 * SPAN
STEPS = 3
ENTRIES = 4 * STEPS
EMPTY, DIAG_HI, DIAG_LO = ENTRIES, ENTRIES + 1, ENTRIES + 2
AROUND = (1, 3, 2)


def dot(a, b, dims=NN):
    return lax.dot_general(a, b, dims, preferred_element_type=F32)


def kernel(q, do, o, norm, k, v, order, segment, wk, wv, dq_out, dk_out, dv_out, kg, wg, *scratch):
    names = [n for n, _ in SCRATCH]
    s = dict(zip(names, scratch))
    qs, ds = [s[f"qs{i}"] for i in range(4)], [s[f"ds{i}"] for i in range(4)]
    qt, dt = [s[f"qt{i}"] for i in range(4)], [s[f"dt{i}"] for i in range(4)]
    nrm, dlt = [s[f"nrm{i}"] for i in range(4)], [s[f"dlt{i}"] for i in range(4)]
    dqa = [s[f"dqa{i}"] for i in range(4)]
    nd = [s["nd0"], s["nd1"]]
    tab, tabz = s["tab"], s["tabz"]
    kb, vb, acck, accv = [s["kb0"], s["kb1"]], [s["vb0"], s["vb1"]], s["acck"], s["accv"]
    bk = [[s[f"bk{g}{half}"] for half in range(2)] for g in range(2)]
    bv = [[s[f"bv{g}{half}"] for half in range(2)] for g in range(2)]
    pos_lo, pos_hi, ent, vis, turn = s["pos_lo"], s["pos_hi"], s["ent"], s["vis"], s["turn"]

    ctx, head = lax.axis_index("ctx"), lax.axis_index("head")
    z, y, x = ctx // 16, (ctx // 4) % 4, ctx % 4
    me = y * 4 + x

    def at_x(d):
        return (z * 16 + y * 4 + (x + d) % 4, head)

    def at_y(d):
        return (z * 16 + ((y + d) % 4) * 4 + x, head)

    over = ((1 - z) * 16 + me, head)
    mate = head + 1 - 2 * (head % 2)
    far, far_mate = (head + 2) % 4, 3 - head
    weight_peers = ((ctx, mate), ((1 - z) * 16 + me, far), ((1 - z) * 16 + me, far_mate))

    barrier = pltpu.get_barrier_semaphore()
    peers = [at_x(d) for d in AROUND] + [at_y(d) for d in AROUND] + [over]
    peers += [weight_peers[0], weight_peers[1], weight_peers[2], (ctx, far)]
    for peer in peers:
        pl.semaphore_signal(barrier, inc=1, device_id=peer, device_id_type=MESH)

    sent = []

    def copy(src, dst, send, recv, peer):
        return pltpu.make_async_remote_copy(
            src_ref=src, dst_ref=dst, send_sem=send, recv_sem=recv, device_id=peer, device_id_type=MESH
        )

    def push(src, dst, send, recv, peer):
        c = copy(src, dst, send, recv, peer)
        c.start()
        sent.append(c)

    def arrived(dst, send, recv):
        copy(dst, dst, send, recv, over).wait_recv()

    def swapped(sel, first, second):
        shape = first.shape
        turn_round = jnp.full(shape, order[0], I32) > jnp.full(shape, order[1], I32)
        return jnp.where(turn_round, second, first) if sel == 0 else jnp.where(turn_round, first, second)

    slots = (pl.ds(0, SPAN), pl.ds(SPAN, SPAN))

    for sel in range(2):
        kb[0][2 * x + sel] = swapped(sel, k[slots[0], :], k[slots[1], :])
        vb[0][2 * x + sel] = swapped(sel, v[slots[0], :], v[slots[1], :])
    for i, value in enumerate((order[0], order[1], segment[0], segment[1])):
        tab[me, 0, i] = value

    def stack(p):
        for sel in range(2):
            for hh in range(4):
                r = pl.ds(hh * SPAN, SPAN)
                c = pl.ds((p * 4 + hh) * HEAD_DIM, HEAD_DIM)
                qs[p][sel, r, :] = swapped(sel, q[slots[0], c], q[slots[1], c])
                ds[p][sel, r, :] = swapped(sel, do[slots[0], c], do[slots[1], c])

    stack(0)
    stack(1)
    pl.semaphore_wait(barrier, len(peers))

    ks, vs = s["k_send"], s["v_send"]
    kr, vr = s["k_recv"], s["v_recv"]
    ms, mr, mrow = s["m_send"], s["m_recv"], s["m_row"]

    def block(buf, r, u):
        return buf[r // 2].at[pl.ds(2 * (r % 2 * 4 + u), 2)]

    def along_x(buf, r, u, send, recv, d):
        push(block(buf, r, u), block(buf, r, u), send, recv.at[r * 4 + u], at_x(d))

    def along_y(buf, r, u, send, recv, d):
        there = (r + 4 - d) % 4
        push(block(buf, r, u), block(buf, there, u), send, recv.at[there * 4 + u], at_y(d))

    for i, d in enumerate(AROUND):
        push(tab.at[me], tab.at[me], ms.at[i], mr.at[me], at_x(d))
    for i, d in enumerate((1, 3)):
        along_x(kb, 0, x, ks.at[i], kr, d)
        along_y(vb, 0, x, vs.at[i], vr, d)
    along_x(kb, 0, x, ks.at[2], kr, 2)
    for i, d in enumerate(AROUND):
        along_x(vb, 0, x, vs.at[3 + i], vr, d)
    for i, d in enumerate((3, 1)):
        along_y(kb, 0, x, ks.at[3 + i], kr, d)
    zs, zr = s["z_send"], s["z_recv"]
    push(tab.at[me], tabz.at[0], ms.at[6], s["mz_recv"].at[0], over)
    push(qs[0], qs[2], zs.at[0], zr.at[0], over)
    push(ds[0], ds[2], zs.at[1], zr.at[1], over)
    ws, wr = s["w_send"], s["w_recv"]
    columns = wk.shape[0] // 4

    def weight_copy(i, w, j):
        peer = weight_peers[j]
        rows = pl.ds(pl.multiple_of(peer[1] * columns, columns), columns)
        return copy(w.at[rows], wg.at[i, head], ws.at[3 * i + j], wr.at[4 * i + head], peer)

    for i, w in enumerate((wk, wv)):
        for j in range(3):
            weight_copy(i, w, j).start()

    fill = []

    lane = lax.broadcasted_iota(I32, (2 * SPAN, 128), 1)
    sums = jnp.zeros((2 * SPAN, 128), F32)
    for h in range(GROUP):
        c = pl.ds(h * HEAD_DIM, HEAD_DIM)
        term = jnp.sum(do[:, c].astype(F32) * o[:, c].astype(F32), axis=1, keepdims=True)
        sums = jnp.where(lane == h, term, sums)
    sums = sums.T[0:8, :]
    for sel in range(2):
        c = pl.ds(sel * SPAN, SPAN)
        nd[0][0:8, c] = swapped(sel, norm[:, slots[0]], norm[:, slots[1]])
        nd[0][8:16, c] = swapped(sel, sums[:, :SPAN], sums[:, SPAN:])
    push(nd[0], nd[1], zs.at[2], zr.at[2], over)
    push(qs[1], qs[3], zs.at[3], zr.at[3], over)
    push(ds[1], ds[3], zs.at[4], zr.at[4], over)

    def spread(g):
        rows = jnp.concatenate([nd[g][...], jnp.zeros((112, 2 * SPAN), F32)], axis=0).T
        for p in range(2):
            for sel in range(2):
                part = rows[sel * SPAN : (sel + 1) * SPAN, :]
                for hh in range(4):
                    h, r = p * 4 + hh, pl.ds(hh * SPAN, SPAN)
                    nrm[2 * g + p][sel, r, :] = jnp.broadcast_to(part[:, h : h + 1] * LOG2E, (SPAN, 128))
                    dlt[2 * g + p][sel, r, :] = jnp.broadcast_to(part[:, 8 + h : 9 + h], (SPAN, 128))

    def turned(i):
        for sel in range(2):
            for hh in range(4):
                r = pl.ds(hh * SPAN, SPAN)
                qt[i][sel, :, r] = qs[i][sel, r, :].T
                dt[i][sel, :, r] = ds[i][sel, r, :].T

    def step(i, sel, k4, v4, bias=None, mask=None):
        n = k4.shape[0] // 128
        e = dot(qs[i][sel], k4, NT) * (SCALE * LOG2E) - jnp.concatenate([nrm[i][sel]] * n, axis=1)
        if bias is not None:
            e = e + bias
        if mask is not None:
            e = jnp.where(mask, e, HIDDEN)
        attend = jnp.exp2(e)
        grad = dot(ds[i][sel], v4, NT) - jnp.concatenate([dlt[i][sel]] * n, axis=1)
        score = (attend * grad).astype(BF16)
        return score, dot(qt[i][sel], score), dot(dt[i][sel], attend.astype(BF16))

    def bias_row(seen):
        return jnp.concatenate(
            [jnp.where(jnp.full((1, 128), one, I32) > 0, 0.0, HIDDEN) for one in seen], axis=1
        )

    def columns_of(a, u):
        return a[:, u * 128 : (u + 1) * 128]

    spread(0)
    turned(0)
    turned(1)
    for i, d in enumerate(AROUND):
        arrived(tab.at[y * 4 + (x + 4 - d) % 4], ms.at[0], mr.at[y * 4 + (x + 4 - d) % 4])
    for i, d in enumerate(AROUND):
        line = pl.ds(y * 4, 4)
        push(tab.at[line], tab.at[line], ms.at[3 + i], mrow.at[y], at_y(d))
    along_y(vb, 0, x, vs.at[2], vr, 2)
    for i, d in enumerate(AROUND):
        u = (x + 4 - d) % 4
        arrived(block(kb, 0, u), ks.at[0], kr.at[u])
        for n, e in enumerate((3, 1)):
            along_y(kb, 0, u, ks.at[6 + 3 * i + n], kr, e)
        if d != 2:
            r = (1, 3)[i]
            arrived(block(vb, r, x), vs.at[0], vr.at[4 * r + x])
            for n, e in enumerate(AROUND):
                along_x(vb, r, x, vs.at[6 + 3 * i + n], vr, e)

    def hand_on_last():
        along_y(kb, 0, x, ks.at[5], kr, 2)
        for i, d in enumerate(AROUND):
            along_y(kb, 0, (x + 4 - d) % 4, ks.at[8 + 3 * i], kr, 2)
        arrived(block(vb, 2, x), vs.at[0], vr.at[8 + x])
        for n, e in enumerate(AROUND):
            along_x(vb, 2, x, vs.at[12 + n], vr, e)

    row = lax.broadcasted_iota(I32, (PIECE, 128), 0) % SPAN
    below = lax.broadcasted_iota(I32, (PIECE, 128), 1) <= row
    for sel in range(2):
        k1, v1 = kb[0][2 * x + sel], vb[0][2 * x + sel]
        place = DIAG_HI if sel else DIAG_LO
        score, dk0, dv0 = step(0, sel, k1, v1, mask=below)
        dqa[0][sel] = dot(score, k1)
        score, dk1, dv1 = step(1, sel, k1, v1, mask=below)
        dqa[1][sel] = dot(score, k1)
        bk[0][0][place] = dk0 + dk1
        bv[0][0][place] = dv0 + dv1
    for b in (bk, bv):
        for g in range(2):
            for half in range(2):
                b[g][half][EMPTY] = jnp.zeros((128, 128), F32)
    for i in (2, 3):
        dqa[i][...] = jnp.zeros_like(dqa[i])

    def low_span(j):
        return jnp.minimum(tab[j, 0, 0], tab[j, 0, 1])

    def query_spans(t, j):
        first = t[j, 0, 0] < t[j, 0, 1]
        low = jnp.where(first, t[j, 0, 0], t[j, 0, 1])
        return low, jnp.where(first, t[j, 0, 2], t[j, 0, 3]), jnp.where(first, t[j, 0, 3], t[j, 0, 2])

    def device_at(half, n):
        return (y + 2 * half + n // 4) % 4 * 4 + n % 4

    def later_rows(pieces, half, line, seg_hi, fresh):
        k4 = jnp.concatenate([kb[half][8 * line + 2 * u] for u in range(4)], axis=0)
        v4 = jnp.concatenate([vb[half][8 * line + 2 * u] for u in range(4)], axis=0)
        bias = bias_row([low_span(device_at(half, 4 * line + u)) - seg_hi + 1 for u in range(4)])
        dks = dvs = None
        for i in pieces:
            score, dk, dv = step(i, 1, k4, v4, bias=bias)
            dqa[i][1] += dot(score, k4)
            dks, dvs = (dk, dv) if dks is None else (dks + dk, dvs + dv)
        for u in range(4):
            place = 8 * half + 4 * line + u
            if fresh:
                acck[place] = columns_of(dks, u)
                accv[place] = columns_of(dvs, u)
            else:
                acck[place] += columns_of(dks, u)
                accv[place] += columns_of(dvs, u)

    def sorted_rows(pieces, g, half, t):
        which = 2 * g + half
        sel = jnp.where(t >= turn[which], 1, 0)
        k4 = jnp.concatenate([kb[half][ent[which * ENTRIES + 4 * t + u]] for u in range(4)], axis=0)
        v4 = jnp.concatenate([vb[half][ent[which * ENTRIES + 4 * t + u]] for u in range(4)], axis=0)
        bias = bias_row([vis[which * ENTRIES + 4 * t + u] for u in range(4)])
        none = jnp.zeros_like(k4)
        early = jnp.full(k4.shape, sel, I32) == 0
        wide = jnp.concatenate([jnp.where(early, k4, none), jnp.where(early, none, k4)], axis=1)
        dks = dvs = None
        for i in pieces:
            score, dk, dv = step(i, sel, k4, v4, bias=bias)
            both = dot(score, wide)
            dqa[i][0] += both[:, :128]
            dqa[i][1] += both[:, 128:]
            dks, dvs = (dk, dv) if dks is None else (dks + dk, dvs + dv)
        for u in range(4):
            bk[g][half][4 * t + u] = columns_of(dks, u)
            bv[g][half][4 * t + u] = columns_of(dvs, u)

    lo_own, seg_lo_own, seg_hi_own = query_spans(tab, me)
    for r in range(1, 4):
        arrived(tab.at[pl.ds(((y + r) % 4) * 4, 4)], ms.at[0], mrow.at[(y + r) % 4])
    arrived(tabz.at[0], ms.at[0], s["mz_recv"].at[0])
    lo_over, seg_lo_over, seg_hi_over = query_spans(tabz, 0)
    for g, (low, seg_lo, seg_hi) in enumerate(
        ((lo_own, seg_lo_own, seg_hi_own), (lo_over, seg_lo_over, seg_hi_over))
    ):
        for half in range(2):
            which = 2 * g + half
            spans = [low_span(device_at(half, n)) for n in range(8)]
            before = sum(jnp.where(one < low, 1, 0) for one in spans)
            upto = sum(jnp.where(one <= low, 1, 0) for one in spans)
            first = (before + 3) // 4
            turn[which] = first

            def place(n, _, half=half, which=which, low=low, spans=spans, upto=upto, first=first):
                mine = low_span(device_at(half, n))
                rank = sum(jnp.where(one < mine, 1, 0) for one in spans)
                hi = 4 * first + rank - upto
                pos_lo[8 * which + n] = jnp.where(mine < low, rank, jnp.where(mine == low, DIAG_LO, EMPTY))
                pos_hi[8 * which + n] = jnp.where(mine > low, hi, jnp.where(mine == low, DIAG_HI, EMPTY))
                return 0

            lax.fori_loop(0, 8, place, 0)

            def entry(p, _, which=which, spans=spans, first=first, seg_lo=seg_lo, seg_hi=seg_hi):
                index, span = jnp.int32(0), jnp.int32(-1)
                for n in range(8):
                    is_lo, is_hi = pos_lo[8 * which + n] == p, pos_hi[8 * which + n] == p
                    index = jnp.where(is_lo, 2 * n, jnp.where(is_hi, 2 * n + 1, index))
                    span = jnp.where(is_lo, spans[n], jnp.where(is_hi, 63 - spans[n], span))
                seg = jnp.where(p < 4 * first, seg_lo, seg_hi)
                ent[which * ENTRIES + p] = index
                vis[which * ENTRIES + p] = jnp.where(span >= seg, 1, 0)
                return 0

            lax.fori_loop(0, ENTRIES, entry, 0)

    for half in range(2):

        def own_line(line, _, half=half):
            r = 2 * half + line
            for u in range(4):
                place = pl.ds(2 * (line * 4 + u), 2)

                if r > 0:
                    arrived(kb[half].at[place], ks.at[0], kr.at[4 * r + u])

                @pl.when(x != u)
                def _():
                    arrived(vb[half].at[place], vs.at[0], vr.at[4 * r + u])

            later_rows((0, 1), half, line, seg_hi_own, True)
            return 0

        if half == 0:
            own_line(0, 0)
            hand_on_last()
            own_line(1, 0)
        else:
            own_line(1, 0)
            own_line(0, 0)

        def own_sorted(t, _, half=half):
            sorted_rows((0, 1), 0, half, t)
            return 0

        lax.fori_loop(0, STEPS, own_sorted, 0)

    dqs, dqr = [s["dqs0"], s["dqs1"]], [s["dqr0"], s["dqr1"]]
    arrived(nd[1], zs.at[0], zr.at[2])
    spread(1)
    for p in range(2):
        arrived(qs[2 + p], zs.at[0], zr.at[3 * p])
        arrived(ds[2 + p], zs.at[0], zr.at[3 * p + 1])
        turned(2 + p)

    def total(acc, b, half, n):
        lo = acc[8 * half + n] + b[0][half][pos_lo[8 * half + n]] + b[1][half][pos_lo[16 + 8 * half + n]]
        hi = b[0][half][pos_hi[8 * half + n]] + b[1][half][pos_hi[16 + 8 * half + n]]
        return jnp.concatenate([lo, hi], axis=1).astype(BF16)

    sk, sv, r1k, r1v = s["sk"], s["sv"], s["r1k"], s["r1v"]
    s1k, s1v, s1kr, s1vr = s["s1k"], s["s1v"], s["s1kr"], s["s1vr"]

    def key_copy(d):
        return copy(sk.at[pl.ds(d * 4, 4)], r1k.at[d - 1], s1k.at[d - 1], s1kr.at[d - 1], at_y(d))

    def value_copy(d, r):
        n = (d - 1) * 4 + r
        return copy(sv.at[r * 4 + (x + d) % 4], r1v.at[d - 1, r], s1v.at[n], s1vr.at[n], at_x(d))

    for half in (1, 0):

        def over_sorted(t, _, half=half):
            sorted_rows((2, 3), 1, half, t)
            return 0

        lax.fori_loop(0, STEPS, over_sorted, 0)

        def over_line(i, _, half=half):
            line = i if half else 1 - i
            r = 2 * half + line
            later_rows((2, 3), half, line, seg_hi_over, False)
            for u in range(4):
                sk[r * 4 + u] = total(acck, bk, half, 4 * line + u)
                sv[r * 4 + u] = total(accv, bv, half, 4 * line + u)

            @pl.when(r > 0)
            def _():
                key_copy(r).start()

            for d in AROUND:
                value_copy(d, r).start()
            return 0

        lax.fori_loop(0, 2, over_line, 0)

    for p in range(2):
        dqs[p][...] = dqa[2 + p][...].astype(BF16)
        push(dqs[p], dqr[p], zs.at[5 + p], zr.at[5 + p], over)

    t2k, t2v, r2k, r2v = s["t2k"], s["t2v"], s["r2k"], s["r2v"]
    for d in (1, 2, 3):
        key_copy(d).wait_recv()

    def sum_keys(u, _):
        parts = sk[u].astype(F32) + r1k[0, u].astype(F32)
        t2k[u] = (parts + r1k[1, u].astype(F32) + r1k[2, u].astype(F32)).astype(BF16)
        return 0

    lax.fori_loop(0, 4, sum_keys, 0)
    for i, d in enumerate(AROUND):
        push(t2k.at[(x + d) % 4], r2k.at[d - 1], s["s2"].at[i], s["s2r"].at[d - 1], at_x(d))

    def value_back(d):
        return copy(t2v.at[d], r2v.at[d - 1], s["s2"].at[2 + d], s["s2r"].at[2 + d], at_y(d))

    def sum_values(i, _):
        r = jnp.where(i < 2, i + 2, 3 - i)
        for d in AROUND:
            value_copy(d, r).wait_recv()
        parts = sv[r * 4 + x].astype(F32) + r1v[0, r].astype(F32)
        t2v[r] = (parts + r1v[1, r].astype(F32) + r1v[2, r].astype(F32)).astype(BF16)

        @pl.when(r > 0)
        def _():
            value_back(r).start()

        return 0

    lax.fori_loop(0, 4, sum_values, 0)

    for p in range(2):
        arrived(dqr[p], zs.at[0], zr.at[5 + p])
        for hh in range(4):
            r, c = pl.ds(hh * SPAN, SPAN), pl.ds((p * 4 + hh) * HEAD_DIM, HEAD_DIM)
            both = [(dqa[p][sel, r, :] + dqr[p][sel, r, :].astype(F32)) * SCALE for sel in range(2)]
            for slot in range(2):
                dq_out[slots[slot], c] = swapped(slot, both[0], both[1]).astype(BF16)

    fin = s["fin"]
    for w, (t2, r2, mine, out, scale) in enumerate(
        ((t2k, r2k, x, dk_out, SCALE), (t2v, r2v, 0, dv_out, 1.0))
    ):
        for d in range(3):
            arrived(r2.at[d], s["s2"].at[0], s["s2r"].at[3 * w + d])
        whole = t2[mine].astype(F32) + r2[0].astype(F32) + r2[1].astype(F32) + r2[2].astype(F32)
        both = [(columns_of(whole, sel) * scale).T for sel in range(2)]
        for slot in range(2):
            low = swapped(slot, both[0], both[1]).astype(BF16)
            out[slots[slot], :] = low
            fin[w, slots[slot], :] = low
        fill.append(pltpu.make_async_copy(fin.at[w], kg.at[w, head], s["fill"].at[w]))
        fill[-1].start()
        for i, peer in enumerate(((ctx, far), (ctx, mate))):
            push(fin.at[w], kg.at[w, head], s["g_send"].at[3 * w + i], s["g_recv"].at[4 * w + head], peer)
    for w in range(2):
        arrived(kg.at[w, far], ws.at[0], s["g_recv"].at[4 * w + far])
        push(kg.at[w, far], kg.at[w, far], s["g_send"].at[3 * w + 2], s["g_recv"].at[4 * w + far], (ctx, mate))

    for w in range(2):
        for h in (mate, far_mate):
            arrived(kg.at[w, h], ws.at[0], s["g_recv"].at[4 * w + h])
        for j, h in enumerate((mate, far, far_mate)):
            arrived(wg.at[w, h], ws.at[0], wr.at[4 * w + h])
            weight_copy(w, (wk, wv)[w], j).wait_send()
    for c in fill:
        c.wait()
    for c in sent:
        c.wait_send()
    for d in (1, 2, 3):
        key_copy(d).wait_send()
        value_back(d).wait_send()
        for r in range(4):
            value_copy(d, r).wait_send()


TILES = 4


def finish(dq, dk, dv, kg, wg, wk, wv, dq_out, dk_out, dv_out, ig_out, a, b, c, dq_in, dk_in, dv_in, into, out, through):
    handed = ((dq, dq_in, dq_out), (dk, dk_in, dk_out), (dv, dv_in, dv_out))
    inward = [pltpu.make_async_copy(src, via, through.at[i]) for i, (src, via, _) in enumerate(handed)]
    onward = [pltpu.make_async_copy(via, dst, through.at[3 + i]) for i, (_, via, dst) in enumerate(handed)]
    first = pltpu.make_async_copy(kg, a, into.at[TILES, 0])
    first.start()
    cols = b.shape[2] // TILES
    head = lax.axis_index("head")
    loads = []
    for n in range(TILES):
        r = pl.ds(n * cols, cols)
        own = pl.ds(pl.multiple_of(head * b.shape[2] + n * cols, cols), cols)
        part = [pltpu.make_async_copy(w.at[own], b.at[i, head, r], into.at[n, i]) for i, w in enumerate((wk, wv))]
        for i in range(2):
            for j in range(1, 4):
                h = (head + j) % 4
                part.append(pltpu.make_async_copy(wg.at[i, h, r], b.at[i, h, r], into.at[n, 2 + 3 * i + j - 1]))
        loads.append(part)
    for one in sum(loads, []) + inward:
        one.start()
    first.wait()
    stores = []
    for n in range(TILES):
        for one in loads[n]:
            one.wait()
        r = pl.ds(n * cols, cols)
        acc = None
        for w in range(2):
            for h in (0, 2):
                left = jnp.concatenate([a[w, h], a[w, h + 1]], axis=1)
                right = jnp.concatenate([b[w, h, r, :], b[w, h + 1, r, :]], axis=1)
                term = dot(left, right, NT)
                acc = term if acc is None else acc + term
        c[:, r] = acc.astype(BF16)
        stores.append(pltpu.make_async_copy(c.at[:, r], ig_out.at[:, r], out.at[n]))
        stores[-1].start()
        if n < 3:
            inward[n].wait()
            onward[n].start()
    for one in stores + onward:
        one.wait()


def _scratch():
    v, dma, smem = pltpu.VMEM, pltpu.SemaphoreType.DMA, pltpu.SMEM
    out = []
    for i in range(4):
        out += [(f"qs{i}", v((2, PIECE, 128), BF16)), (f"ds{i}", v((2, PIECE, 128), BF16))]
        out += [(f"qt{i}", v((2, 128, PIECE), BF16)), (f"dt{i}", v((2, 128, PIECE), BF16))]
        out += [(f"nrm{i}", v((2, PIECE, 128), F32)), (f"dlt{i}", v((2, PIECE, 128), F32))]
        out += [(f"dqa{i}", v((2, PIECE, 128), F32))]
    for i in range(2):
        out += [(f"nd{i}", v((16, 256), F32)), (f"dqs{i}", v((2, PIECE, 128), BF16))]
        out += [(f"dqr{i}", v((2, PIECE, 128), BF16))]
        for half in range(2):
            out += [(f"b{n}{i}{half}", v((ENTRIES + 3, 128, 128), F32)) for n in ("k", "v")]
            out += [(f"{n}b{half}", v((16, 128, 128), BF16)) for n in ("k", "v") if i == 0]
    out += [("tab", smem((16, 1, 128), I32)), ("tabz", smem((1, 1, 128), I32))]
    out += [("acck", v((16, 128, 128), F32)), ("accv", v((16, 128, 128), F32))]
    out += [("pos_lo", smem((32,), I32)), ("pos_hi", smem((32,), I32)), ("ent", smem((4 * ENTRIES,), I32))]
    out += [("vis", smem((4 * ENTRIES,), I32)), ("turn", smem((4,), I32))]
    out += [("sk", v((16, 128, 256), BF16)), ("sv", v((16, 128, 256), BF16))]
    for n in ("k", "v"):
        out += [(f"r1{n}", v((3, 4, 128, 256), BF16))]
        out += [(f"t2{n}", v((4, 128, 256), BF16)), (f"r2{n}", v((3, 128, 256), BF16))]
    out += [("fin", v((2, 256, 128), BF16))]
    out += [("k_send", dma((15,))), ("v_send", dma((15,))), ("k_recv", dma((16,))), ("v_recv", dma((16,)))]
    out += [("m_send", dma((7,))), ("m_recv", dma((16,))), ("m_row", dma((4,))), ("mz_recv", dma((1,)))]
    out += [("z_send", dma((7,))), ("z_recv", dma((7,))), ("w_send", dma((6,))), ("w_recv", dma((8,)))]
    out += [("fill", dma((2,))), ("s1k", dma((3,))), ("s1kr", dma((3,))), ("s1v", dma((12,))), ("s1vr", dma((12,)))]
    out += [("s2", dma((6,))), ("s2r", dma((6,)))]
    out += [("g_send", dma((6,))), ("g_recv", dma((8,)))]
    return out


SCRATCH = _scratch()


def per_device(
    query, key, value, attention_out, out_grad, log_norm, span_order, span_segment, key_weight, value_weight
):
    rows = query.shape[0]
    vmem, smem = pl.BlockSpec(memory_space=pltpu.VMEM), pl.BlockSpec(memory_space=pltpu.SMEM)
    hbm = pl.BlockSpec(memory_space=pl.ANY)
    columns = key_weight.shape[0] // 4
    small = (
        jax.ShapeDtypeStruct(query.shape, BF16),
        jax.ShapeDtypeStruct(key.shape, BF16),
        jax.ShapeDtypeStruct(value.shape, BF16),
    )
    held = pl.pallas_call(
        kernel,
        name="attention_backward",
        out_shape=small
        + (
            jax.ShapeDtypeStruct((2, 4, rows, HEAD_DIM), BF16),
            jax.ShapeDtypeStruct((2, 4, columns, HEAD_DIM), BF16),
        ),
        in_specs=[vmem] * 6 + [smem] * 2 + [hbm] * 2,
        out_specs=(vmem,) * 3 + (hbm,) * 2,
        scratch_shapes=[shape for _, shape in SCRATCH],
        compiler_params=pltpu.CompilerParams(
            collective_id=0, has_side_effects=True, vmem_limit_bytes=60 << 20
        ),
        cost_estimate=pl.CostEstimate(flops=11_000_000_000, bytes_accessed=16 << 20, transcendentals=0),
    )(
        query, out_grad, attention_out, log_norm.T, key, value,
        span_order, span_segment, key_weight, value_weight,
    )
    dma = pltpu.SemaphoreType.DMA
    return pl.pallas_call(
        finish,
        name="input_gradient",
        out_shape=small + (jax.ShapeDtypeStruct((rows, columns), BF16),),
        in_specs=[hbm] * 7,
        out_specs=(hbm,) * 4,
        scratch_shapes=[
            pltpu.VMEM((2, 4, rows, HEAD_DIM), BF16),
            pltpu.VMEM((2, 4, columns, HEAD_DIM), BF16),
            pltpu.VMEM((rows, columns), BF16),
            pltpu.VMEM(query.shape, BF16),
            pltpu.VMEM(key.shape, BF16),
            pltpu.VMEM(value.shape, BF16),
            dma((TILES + 1, 8)),
            dma((TILES,)),
            dma((6,)),
        ],
        compiler_params=pltpu.CompilerParams(vmem_limit_bytes=60 << 20),
        cost_estimate=pl.CostEstimate(flops=1_100_000_000, bytes_accessed=8 << 20, transcendentals=0),
    )(*held, key_weight, value_weight)


def solution(mesh):
    split = P("ctx", "head")
    in_specs = (split,) * 6 + (P("ctx"), P("ctx"), P(None, "head"), P(None, "head"))
    return jax.shard_map(
        per_device, mesh=mesh, in_specs=in_specs, out_specs=(split,) * 4, check_vma=False
    )
```

time: 81.3 us -> 77.6 us (0.954)
  Pallas kernels: 79.8 us -> 76.7 us
    pallas_call x1, Pallas kernels: 6.19 us -> 4.6 us  [per_device(): pl.pallas_call(finish, name='input_gradient', out_shape=small + (jax.Shap...]
    pallas_call x1, Pallas kernels: 73.6 us -> 72.1 us  [per_device(): pl.pallas_call(kernel, name='attention_backward', out_shape=small + (jax....]
where the time goes in v3:
time: 77.6 us; the launch traced here: 77.5 us
  Pallas kernels  76.7 us (99%)
  between operations  0.82 us (1%)
    pallas_call x1, Pallas kernels, per_device(): pl.pallas_call(kernel, name='attention_backward', out_shape=small + (jax....  72.1 us
    pallas_call x1, Pallas kernels, per_device(): pl.pallas_call(finish, name='input_gradient', out_shape=small + (jax.Shap...  4.6 us

profile of v3, /device:TPU:1, one launch (start us, length us, event | category | flops | bytes accessed | tf_op | source)
XLA Modules:
  0.0 77.5 jit_solution(3036573310217871734)
XLA Ops:
  0.6 72.1 %attention_backward.1 = (bf16[256,1024]{1,0:T(8,128)(2,1)}, bf16[256,128]{1,0:T(8,128)(2,1)}, bf16[256,128]{1,0:T(8,128)(2,1)}, bf16[2,4,256,128]{3,2,1,0:T(8,128)(2,1)}, bf16[2,4,2048,128]{3,2,1,0:T(8,128)(2,1)}) custom-call(bf16[256,1024]{1,0:T(8,128)(2,1)} %q.1, bf16[256,1024]{1,0:T(8,128)(2,1)} %do.1, bf16[256,1024]{1,0:T(8,128)(2,1)} %o.1, ...), custom_call_target="tpu_custom_call" | custom-call | flops 11000000512 | bytes 16777216 | tf_op jit(solution)/shard_map/attention_backward/pallas_call | solution.py:587
  72.7 4.6 %input_gradient.1 = (bf16[256,1024]{1,0:T(8,128)(2,1)}, bf16[256,128]{1,0:T(8,128)(2,1)}, bf16[256,128]{1,0:T(8,128)(2,1)}, bf16[256,2048]{1,0:T(8,128)(2,1)}) custom-call(bf16[256,1024]{1,0:T(8,128)(2,1)} %get-tuple-element.9.dq, bf16[256,128]{1,0:T(8,128)(2,1)} %get-tuple-element.10.dk, bf16[256,128]{1,0:T(8,128)(2,1)} %get-tuple-element.11.dv, ...), custom_call_target="tpu_custom_call" | custom-call | flops 1100000000 | bytes 8388608 | tf_op jit(solution)/shard_map/input_gradient/pallas_call | solution.py:607

commit v4 on v3

--- a/solution.py
+++ b/solution.py
@@ -360,7 +360,7 @@
             sorted_rows((0, 1), 0, half, t)
             return 0
 
-        lax.fori_loop(0, STEPS, own_sorted, 0)
+        lax.fori_loop(0, STEPS, own_sorted, 0, unroll=True)
 
     dqs, dqr = [s["dqs0"], s["dqs1"]], [s["dqr0"], s["dqr1"]]
     arrived(nd[1], zs.at[0], zr.at[2])
@@ -391,7 +391,7 @@
             sorted_rows((2, 3), 1, half, t)
             return 0
 
-        lax.fori_loop(0, STEPS, over_sorted, 0)
+        lax.fori_loop(0, STEPS, over_sorted, 0, unroll=True)
 
         def over_line(i, _, half=half):
             line = i if half else 1 - i
@@ -416,6 +416,20 @@
         push(dqs[p], dqr[p], zs.at[5 + p], zr.at[5 + p], over)
 
     t2k, t2v, r2k, r2v = s["t2k"], s["t2v"], s["r2k"], s["r2v"]
+
+    def value_back(d):
+        return copy(t2v.at[d], r2v.at[d - 1], s["s2"].at[2 + d], s["s2r"].at[2 + d], at_y(d))
+
+    def sum_values(r):
+        for d in AROUND:
+            value_copy(d, r).wait_recv()
+        parts = sv[r * 4 + x].astype(F32) + r1v[0, r].astype(F32)
+        t2v[r] = (parts + r1v[1, r].astype(F32) + r1v[2, r].astype(F32)).astype(BF16)
+        if r:
+            value_back(r).start()
+
+    for r in (2, 3, 1):
+        sum_values(r)
     for d in (1, 2, 3):
         key_copy(d).wait_recv()
 
@@ -427,24 +441,7 @@
     lax.fori_loop(0, 4, sum_keys, 0)
     for i, d in enumerate(AROUND):
         push(t2k.at[(x + d) % 4], r2k.at[d - 1], s["s2"].at[i], s["s2r"].at[d - 1], at_x(d))
-
-    def value_back(d):
-        return copy(t2v.at[d], r2v.at[d - 1], s["s2"].at[2 + d], s["s2r"].at[2 + d], at_y(d))
-
-    def sum_values(i, _):
-        r = jnp.where(i < 2, i + 2, 3 - i)
-        for d in AROUND:
-            value_copy(d, r).wait_recv()
-        parts = sv[r * 4 + x].astype(F32) + r1v[0, r].astype(F32)
-        t2v[r] = (parts + r1v[1, r].astype(F32) + r1v[2, r].astype(F32)).astype(BF16)
-
-        @pl.when(r > 0)
-        def _():
-            value_back(r).start()
-
-        return 0
-
-    lax.fori_loop(0, 4, sum_values, 0)
+    sum_values(0)
 
     for p in range(2):
         arrived(dqr[p], zs.at[0], zr.at[5 + p])

time: 77.6 us -> 74.1 us (0.955)
  Pallas kernels: 76.7 us -> 73.1 us
    pallas_call x1, Pallas kernels: 72.1 us -> 68.5 us  [per_device(): pl.pallas_call(kernel, name='attention_backward', out_shape=small + (jax....]
where the time goes in v4:
time: 74.1 us; the launch traced here: 74 us
  Pallas kernels  73.1 us (99%)
  between operations  0.82 us (1%)
    pallas_call x1, Pallas kernels, per_device(): pl.pallas_call(kernel, name='attention_backward', out_shape=small + (jax....  68.5 us
    pallas_call x1, Pallas kernels, per_device(): pl.pallas_call(finish, name='input_gradient', out_shape=small + (jax.Shap...  4.6 us

profile of v4, /device:TPU:1, one launch (start us, length us, event | category | flops | bytes accessed | tf_op | source)
XLA Modules:
  0.0 74.0 jit_solution(4819480998961234256)
XLA Ops:
  0.6 68.5 %attention_backward.1 = (bf16[256,1024]{1,0:T(8,128)(2,1)}, bf16[256,128]{1,0:T(8,128)(2,1)}, bf16[256,128]{1,0:T(8,128)(2,1)}, bf16[2,4,256,128]{3,2,1,0:T(8,128)(2,1)}, bf16[2,4,2048,128]{3,2,1,0:T(8,128)(2,1)}) custom-call(bf16[256,1024]{1,0:T(8,128)(2,1)} %q.1, bf16[256,1024]{1,0:T(8,128)(2,1)} %do.1, bf16[256,1024]{1,0:T(8,128)(2,1)} %o.1, ...), custom_call_target="tpu_custom_call" | custom-call | flops 11000000512 | bytes 16777216 | tf_op jit(solution)/shard_map/attention_backward/pallas_call | solution.py:584
  69.2 4.6 %input_gradient.1 = (bf16[256,1024]{1,0:T(8,128)(2,1)}, bf16[256,128]{1,0:T(8,128)(2,1)}, bf16[256,128]{1,0:T(8,128)(2,1)}, bf16[256,2048]{1,0:T(8,128)(2,1)}) custom-call(bf16[256,1024]{1,0:T(8,128)(2,1)} %get-tuple-element.9.dq, bf16[256,128]{1,0:T(8,128)(2,1)} %get-tuple-element.10.dk, bf16[256,128]{1,0:T(8,128)(2,1)} %get-tuple-element.11.dv, ...), custom_call_target="tpu_custom_call" | custom-call | flops 1100000000 | bytes 8388608 | tf_op jit(solution)/shard_map/input_gradient/pallas_call | solution.py:604

commit v5 on v4

--- a/solution.py
+++ b/solution.py
@@ -100,7 +100,6 @@
                 ds[p][sel, r, :] = swapped(sel, do[slots[0], c], do[slots[1], c])
 
     stack(0)
-    stack(1)
     pl.semaphore_wait(barrier, len(peers))
 
     ks, vs = s["k_send"], s["v_send"]
@@ -145,6 +144,7 @@
 
     fill = []
 
+    stack(1)
     lane = lax.broadcasted_iota(I32, (2 * SPAN, 128), 1)
     sums = jnp.zeros((2 * SPAN, 128), F32)
     for h in range(GROUP):
@@ -443,14 +443,6 @@
         push(t2k.at[(x + d) % 4], r2k.at[d - 1], s["s2"].at[i], s["s2r"].at[d - 1], at_x(d))
     sum_values(0)
 
-    for p in range(2):
-        arrived(dqr[p], zs.at[0], zr.at[5 + p])
-        for hh in range(4):
-            r, c = pl.ds(hh * SPAN, SPAN), pl.ds((p * 4 + hh) * HEAD_DIM, HEAD_DIM)
-            both = [(dqa[p][sel, r, :] + dqr[p][sel, r, :].astype(F32)) * SCALE for sel in range(2)]
-            for slot in range(2):
-                dq_out[slots[slot], c] = swapped(slot, both[0], both[1]).astype(BF16)
-
     fin = s["fin"]
     for w, (t2, r2, mine, out, scale) in enumerate(
         ((t2k, r2k, x, dk_out, SCALE), (t2v, r2v, 0, dv_out, 1.0))
@@ -467,6 +459,14 @@
         fill[-1].start()
         for i, peer in enumerate(((ctx, far), (ctx, mate))):
             push(fin.at[w], kg.at[w, head], s["g_send"].at[3 * w + i], s["g_recv"].at[4 * w + head], peer)
+    for p in range(2):
+        arrived(dqr[p], zs.at[0], zr.at[5 + p])
+        for hh in range(4):
+            r, c = pl.ds(hh * SPAN, SPAN), pl.ds((p * 4 + hh) * HEAD_DIM, HEAD_DIM)
+            both = [(dqa[p][sel, r, :] + dqr[p][sel, r, :].astype(F32)) * SCALE for sel in range(2)]
+            for slot in range(2):
+                dq_out[slots[slot], c] = swapped(slot, both[0], both[1]).astype(BF16)
+
     for w in range(2):
         arrived(kg.at[w, far], ws.at[0], s["g_recv"].at[4 * w + far])
         push(kg.at[w, far], kg.at[w, far], s["g_send"].at[3 * w + 2], s["g_recv"].at[4 * w + far], (ctx, mate))

time: 74.1 us -> 73.6 us (level)
  no operation moved by 1% of the time
where the time goes in v5:
time: 73.6 us; the launch traced here: 73.4 us
  Pallas kernels  72.6 us (99%)
  between operations  0.82 us (1%)
    pallas_call x1, Pallas kernels, per_device(): pl.pallas_call(kernel, name='attention_backward', out_shape=small + (jax....  68 us
    pallas_call x1, Pallas kernels, per_device(): pl.pallas_call(finish, name='input_gradient', out_shape=small + (jax.Shap...  4.61 us

profile of v5, /device:TPU:1, one launch (start us, length us, event | category | flops | bytes accessed | tf_op | source)
XLA Modules:
  0.0 73.4 jit_solution(1931259546838144796)
XLA Ops:
  0.6 68.0 %attention_backward.1 = (bf16[256,1024]{1,0:T(8,128)(2,1)}, bf16[256,128]{1,0:T(8,128)(2,1)}, bf16[256,128]{1,0:T(8,128)(2,1)}, bf16[2,4,256,128]{3,2,1,0:T(8,128)(2,1)}, bf16[2,4,2048,128]{3,2,1,0:T(8,128)(2,1)}) custom-call(bf16[256,1024]{1,0:T(8,128)(2,1)} %q.1, bf16[256,1024]{1,0:T(8,128)(2,1)} %do.1, bf16[256,1024]{1,0:T(8,128)(2,1)} %o.1, ...), custom_call_target="tpu_custom_call" | custom-call | flops 11000000512 | bytes 16777216 | tf_op jit(solution)/shard_map/attention_backward/pallas_call | solution.py:584
  68.6 4.6 %input_gradient.1 = (bf16[256,1024]{1,0:T(8,128)(2,1)}, bf16[256,128]{1,0:T(8,128)(2,1)}, bf16[256,128]{1,0:T(8,128)(2,1)}, bf16[256,2048]{1,0:T(8,128)(2,1)}) custom-call(bf16[256,1024]{1,0:T(8,128)(2,1)} %get-tuple-element.9.dq, bf16[256,128]{1,0:T(8,128)(2,1)} %get-tuple-element.10.dk, bf16[256,128]{1,0:T(8,128)(2,1)} %get-tuple-element.11.dv, ...), custom_call_target="tpu_custom_call" | custom-call | flops 1100000000 | bytes 8388608 | tf_op jit(solution)/shard_map/input_gradient/pallas_call | solution.py:604
